TPU v7x, 512 devices: a whole 4x4x16 slice. The times are simulated.
512 devices in a mesh: row: 16 (over z), col: 32 (over x, y, core).
Axes of the slice: x: 4, y: 4, z: 16, core: 2. Of those that a mesh axis runs over, the one named last changes fastest.
Arguments:
- band: float32 [2, 512, 65536], P(None, 'row', 'col'), may hold values from -6 to 6
- sources: int32 [512, 4], P('row'), may hold values from 0 to 511, as said below
- taps: float32 [512, 4], P('row'), may hold values from 0.1 to 1
- jacobian: float32 [512, 65536], P('row', 'col'), may hold values from 0.3 to 3
- phase: float32 [512, 65536], P('row', 'col'), may hold values from -3.140625 to 3.140625
Outputs:
- tilted: float32 [2, 512, 65536], P(None, 'row', 'col')
Inputs may be any that keep to these rules, and one draw needn't show every extreme that they name: Row r's sources are four consecutive rows b, b + 1, b + 2, b + 3 with r - 16 <= b and b + 3 <= r + 16.
All inputs are finite; a program needn't handle non-finite values.
Results may differ from a plain program's by a relative error of at most 0.00007.
Values sent between devices are 32-bit elements; how exact they have to be, the bound alone decides.
No kernel may reach another device: no remote copies, remote signals or barrier semaphores. Data moves between devices by JAX's collectives and lax.ppermute only.
A program may use at most 192 MiB of HBM per device.

v0:
```python
import math

import jax
import jax.numpy as jnp
from jax import lax
from jax.sharding import PartitionSpec as P

W1 = 256


def extended_2(value, sides, width):
    for axis, dim in sides:
        size, length = (lax.axis_size(axis), value.shape[dim])
        up = [(i, (i + 1) % size) for i in range(size - 1)]
        down = [(j, i) for i, j in up]
        last = lax.slice_in_dim(value, length - width, length, axis=dim)
        initial = lax.slice_in_dim(value, 0, width, axis=dim)
        before = lax.ppermute(last, axis, up)
        after = lax.ppermute(initial, axis, down)
        value = jnp.concatenate([before, value, after], axis=dim)
    return value


def angles(left, right, period):
    product = left[:, None] * right[None, :] % period
    return -2.0 * math.pi / period * product.astype(jnp.float32)


def section_tables(width):
    second = width // W1
    first_idx = jnp.arange(W1, dtype=jnp.int32)
    second_idx = jnp.arange(second, dtype=jnp.int32)
    ang_first = angles(first_idx, first_idx, W1)
    cos_first = jnp.cos(ang_first)
    sin_first = jnp.sin(ang_first)
    first_table = jnp.stack([jnp.stack([cos_first, -sin_first]), jnp.stack([sin_first, cos_first])])
    twist = angles(first_idx, second_idx, width)
    twist_re = jnp.cos(twist)
    twist_im = jnp.sin(twist)
    ang_second = angles(second_idx, second_idx, second)
    scale = 1.0 / math.sqrt(width)
    cos_second = jnp.cos(ang_second) * scale
    sin_second = jnp.sin(ang_second) * scale
    second_table = jnp.stack(
        [jnp.stack([cos_second, sin_second]), jnp.stack([-sin_second, cos_second])]
    )
    return (first_table, twist_re, twist_im, second_table)


def transform_rows(piece, tables):
    first_table, twist_re, twist_im, second_table = tables
    width = piece.shape[-1]
    second = width // W1
    parts = piece.reshape(2, -1, W1, second)
    high = lax.Precision.HIGHEST
    section = jnp.einsum("cdka,dnab->cnkb", first_table, parts, precision=high)
    turned = jnp.stack(
        [
            section[0] * twist_re - section[1] * twist_im,
            section[0] * twist_im + section[1] * twist_re,
        ]
    )
    final = jnp.einsum("cnkb,cebm->enmk", turned, second_table, precision=high)
    return final.reshape(piece.shape)


def transform_band(field):
    ncol = lax.axis_size("col")
    rows_here = field.shape[1]
    cols_here = field.shape[2]
    blocks = field.reshape(2, rows_here // ncol, ncol, cols_here)
    tables = section_tables(ncol * cols_here)
    spectra = transform_rows(
        lax.all_to_all(blocks, "col", split_axis=2, concat_axis=3, tiled=True), tables
    )
    result = lax.all_to_all(spectra, "col", split_axis=3, concat_axis=2, tiled=True)
    return result.reshape(2, rows_here, cols_here)


def remap_rows(extended, sources, taps, rows_here):
    margin = (extended.shape[1] - rows_here) // 2
    start = lax.axis_index("row") * rows_here
    local_src = sources - start + margin
    total = jnp.zeros((2, rows_here, extended.shape[2]), jnp.float32)
    for j in range(4):
        total = total + taps[:, j][None, :, None] * jnp.take(extended, local_src[:, j], axis=1)
    return total


def shards(band, sources, taps, jacobian, phase):
    rows_here = band.shape[1]
    margin = rows_here // 2
    spectra = transform_band(band)
    extended = extended_2(spectra, (("row", 1),), margin)
    remapped = remap_rows(extended, sources, taps, rows_here)
    cosine = jnp.cos(phase)
    sine = jnp.sin(phase)
    out_re = jacobian * (remapped[0] * cosine - remapped[1] * sine)
    out_im = jacobian * (remapped[0] * sine + remapped[1] * cosine)
    return jnp.stack([out_re, out_im])


def solution(mesh):
    placed = (
        P(None, "row", "col"),
        P("row", None),
        P("row", None),
        P("row", "col"),
        P("row", "col"),
    )
    return jax.shard_map(
        shards, mesh=mesh, in_specs=placed, out_specs=P(None, "row", "col"), check_vma=False
    )
```

profile of v0, /device:TPU:96, one launch (start us, length us, event | category | flops | bytes accessed | tf_op | source)
XLA Modules:
  0.0 475.0 jit_solution(12059314926972679131)
XLA Ops:
  0.0 2.2 copy.56
  2.2 7.3 %all-to-all-start = ((f32[2,1,32,2048]{3,0,1,2:T(2,128)}), f32[2,1,32,2048]{3,0,1,2:T(2,128)S(1)}, u32[]{:S(2)}, u32[]{:S(2)}) async-start(f32[2,1,32,2048]{3,0,1,2:T(2,128)} %bitcast.92), calls=%async_computation | async-start | bytes 1048576 | tf_op jit(solution)/shard_map/all_to_all | solution.py:74
  14.5 6.2 %all-to-all-done = f32[2,1,32,2048]{3,0,1,2:T(2,128)S(1)} async-done(((f32[2,1,32,2048]{3,0,1,2:T(2,128)}), f32[2,1,32,2048]{3,0,1,2:T(2,128)S(1)}, u32[]{:S(2)}, u32[]{:S(2)}) %all-to-all-start) | async-done | bytes 524320 | tf_op jit(solution)/shard_map/all_to_all | solution.py:74
  22.1 1.1 multiply_subtract_fusion
  23.3 1.8 convolution_bitcast_fusion
  25.1 16.6 %copy.38 = f32[2,256,256]{0,2,1:T(8,128)} copy(f32[2,256,256]{2,1,0:T(8,128)S(1)} %convolution_bitcast_fusion) | data formatting | bytes 1048576 | tf_op jit(solution)/shard_map/reshape;cnkb,cebm->enmk/transpose | solution.py:64
  42.2 291.1 %reduce = f32[65536,2]{1,0:T(8,128)} reduce(f32[65536,1,1,2]{3,2,1,0:T(1,128)} %bitcast.93, f32[]{:T(128)} %broadcast.401), dimensions={1,2}, to_apply=%bitcast.85.reduce_sub_computation | reduce | bytes 1048580
  333.4 26.8 %reshape.285 = f32[32,1,4096]{2,1,0:T(1,128)} reshape(f32[65536,2]{1,0:T(8,128)} %reduce) | data formatting | bytes 1048576
  360.2 4.1 all-to-all-start.1
  364.3 1.6 fusion.32
  365.9 9.5 %all-to-all-done.1 = f32[32,1,4096]{2,1,0:T(1,128)S(1)} async-done(((f32[32,1,4096]{2,1,0:T(1,128)}), f32[32,1,4096]{2,1,0:T(1,128)S(1)}, u32[]{:S(2)}, u32[]{:S(2)}) %all-to-all-start.1) | async-done | bytes 524320 | tf_op jit(solution)/shard_map/all_to_all | solution.py:76
  375.4 1.9 reduce.1
  377.3 54.7 %reshape.286 = f32[65536,1,1,2]{3,2,1,0:T(1,128)} reshape(f32[32,4096]{1,0:T(8,128)S(1)} %reduce.1) | data formatting | bytes 1048576
  432.0 17.6 %copy.28 = f32[2,32,2048]{2,0,1:T(2,128)S(1)} copy(f32[2,32,2048]{0,2,1:T(8,128)} %bitcast.94) | data formatting | bytes 1048576 | tf_op jit(solution)/shard_map/reshape | solution.py:77
  449.7 5.3 %collective-permute-start = (f32[2,16,2048]{2,0,1:T(2,128)S(1)}, f32[2,16,2048]{2,0,1:T(2,128)S(1)}, u32[]{:S(2)}, u32[]{:S(2)}) collective-permute-start(f32[2,16,2048]{2,0,1:T(2,128)S(1)} %get-tuple-element.16), channel_id=1, source_target_pairs={{0,32},{32,64},{64,96},{96,128},{128,160},{160,192},{192,224},{224... | collective-permute-start | bytes 786440 | tf_op jit(solution)/shard_map/ppermute | solution.py:18
  454.9 1.9 collective-permute-start.1
  456.9 4.4 collective-permute-done
  461.3 5.3 %collective-permute-done.1 = f32[2,16,2048]{2,0,1:T(2,128)S(1)} collective-permute-done((f32[2,16,2048]{2,0,1:T(2,128)S(1)}, f32[2,16,2048]{2,0,1:T(2,128)S(1)}, u32[]{:S(2)}, u32[]{:S(2)}) %collective-permute-start.1) | collective-permute-done | bytes 262176 | tf_op jit(solution)/shard_map/ppermute | solution.py:19
  467.2 1.1 gather_fusion
  468.4 1.1 gather_fusion.1
  469.5 1.1 gather_fusion.2
  470.6 1.1 gather_fusion.3
  471.7 1.4 fusion.8
  473.1 1.9 multiply_bitcast_fusion.1
  (22 shorter events, 7.4 us)
Async XLA Ops:
  2.2 18.5 %all-to-all-start = ((f32[2,1,32,2048]{3,0,1,2:T(2,128)}), f32[2,1,32,2048]{3,0,1,2:T(2,128)S(1)}, u32[]{:S(2)}, u32[]{:S(2)}) async-start(f32[2,1,32,2048]{3,0,1,2:T(2,128)} %bitcast.92), calls=%async_computation | async-start | bytes 1048576 | tf_op jit(solution)/shard_map/all_to_all | solution.py:74
  333.4 30.9 %copy-start = (f32[32,2048]{1,0:T(8,128)S(1)}, f32[32,2048]{1,0:T(8,128)}, u32[]{:S(2)}) copy-start(f32[32,2048]{1,0:T(8,128)} %param.11) | copy-start | bytes 786436
  360.2 15.3 %all-to-all-start.1 = ((f32[32,1,4096]{2,1,0:T(1,128)}), f32[32,1,4096]{2,1,0:T(1,128)S(1)}, u32[]{:S(2)}, u32[]{:S(2)}) async-start(f32[32,1,4096]{2,1,0:T(1,128)} %reshape.285), calls=%async_computation.1 | async-start | bytes 1048576 | tf_op jit(solution)/shard_map/all_to_all | solution.py:76
  377.3 79.6 %copy-start.1 = (f32[32,4]{0,1:T(4,128)S(1)}, f32[32,4]{0,1:T(4,128)}, u32[]{:S(2)}) copy-start(f32[32,4]{0,1:T(4,128)} %param.9) | copy-start | bytes 1540
  449.7 11.7 %collective-permute-start = (f32[2,16,2048]{2,0,1:T(2,128)S(1)}, f32[2,16,2048]{2,0,1:T(2,128)S(1)}, u32[]{:S(2)}, u32[]{:S(2)}) collective-permute-start(f32[2,16,2048]{2,0,1:T(2,128)S(1)} %get-tuple-element.16), channel_id=1, source_target_pairs={{0,32},{32,64},{64,96},{96,128},{128,160},{160,192},{192,224},{224... | collective-permute-start | bytes 786440 | tf_op jit(solution)/shard_map/ppermute | solution.py:18
  454.9 11.8 %collective-permute-start.1 = (f32[2,16,2048]{2,0,1:T(2,128)S(1)}, f32[2,16,2048]{2,0,1:T(2,128)S(1)}, u32[]{:S(2)}, u32[]{:S(2)}) collective-permute-start(f32[2,16,2048]{2,0,1:T(2,128)S(1)} %get-tuple-element.17), channel_id=1, source_target_pairs={{32,0},{64,32},{96,64},{128,96},{160,128},{192,160},{224,192},{256... | collective-permute-start | bytes 786440 | tf_op jit(solution)/shard_map/ppermute | solution.py:19
where the time goes:
time: 476 us; the launch traced here: 475 us
  other arithmetic  303 us (64%)
  local copies, waits for them, and re-layouts  125 us (26%)
  waiting for transfers between devices  25.6 us (5%)
  starting transfers between devices  18.6 us (4%)
    unnamed x1, other arithmetic  291 us
    unnamed x8, local copies, waits for them, and re-layouts  84.3 us
    reshape x1, local copies, waits for them, and re-layouts, transform_band(): return result.reshape(2, rows_here, cols_here)  17.6 us
    transpose x1, local copies, waits for them, and re-layouts, transform_rows(): return final.reshape(piece.shape)  16.6 us
    all_to_all x1, waiting for transfers between devices, transform_band(): lax.all_to_all(spectra, 'col', split_axis=3, concat_axis=2, tiled=True)  9.55 us
  transfers between devices with their start and end apart: 4, of which 4 were waited for; matrix products, arithmetic and copies ran while one was open for 1% of the time, Pallas kernels for 0%

commit v1 on v0

v1 whole, which is shorter than its diff:
```python
import math

import jax
import jax.numpy as jnp
import numpy as np
from jax import lax
from jax.experimental import pallas as pl
from jax.experimental.pallas import tpu as pltpu
from jax.sharding import PartitionSpec as P

N1 = 256
LANES = 128
ROWS = 32
HALO = 16
TILES = 16
SLAB = 32


def split_bf16(x):
    hi = x.astype(jnp.bfloat16)
    lo = (x - hi.astype(jnp.float32)).astype(jnp.bfloat16)
    return hi, lo


def dft_tables():
    idx = np.arange(N1, dtype=np.int64)
    ang = 2.0 * np.pi * ((idx[:, None] * idx[None, :]) % N1) / N1
    cos, sin = np.cos(ang), np.sin(ang)
    table = np.block([[cos, sin], [-sin, cos]])
    hi = table.astype(np.float32).astype(jnp.bfloat16)
    lo = (table - hi.astype(np.float64)).astype(np.float32).astype(jnp.bfloat16)
    twist = -2.0 * np.pi * (idx[:, None] * idx[None, :]) / (N1 * N1)
    scale = 1.0 / N1
    turn = np.stack([np.cos(twist) * scale, np.sin(twist) * scale]).astype(np.float32)
    return hi, lo, turn


def sine_cosine_coefficients():
    nodes = np.cos((np.arange(400) + 0.5) * np.pi / 400) * (np.pi / 2)
    square = nodes * nodes
    sinc = np.where(nodes == 0, 1.0, np.sin(nodes) / nodes)
    powers = np.stack([square**i for i in range(7)], axis=1)
    sine = np.linalg.lstsq(powers, sinc, rcond=None)[0]
    cosine = np.linalg.lstsq(powers, np.cos(nodes), rcond=None)[0]
    return [float(v) for v in sine], [float(v) for v in cosine]


SINE, COSINE = sine_cosine_coefficients()


def polynomial(square, coefficients):
    total = jnp.full_like(square, coefficients[-1])
    for value in coefficients[-2::-1]:
        total = total * square + value
    return total


def sine_cosine(x):
    half = 0.5 * x
    square = half * half
    s = half * polynomial(square, SINE)
    c = polynomial(square, COSINE)
    return 2.0 * s * c, 1.0 - 2.0 * s * s


def slab_kernel(band_ref, out_ref):
    for c in range(2):
        for tile in range(TILES):
            start = c * 16 + (tile % 2) * 8 + tile // 2
            out_ref[pl.ds(start, ROWS, stride=SLAB), :] = band_ref[
                c, :, tile * LANES : (tile + 1) * LANES
            ]


def transform_kernel(in_ref, hi_ref, lo_ref, turn_ref, out_ref):
    def part(c):
        halves = [in_ref[:, c, h].reshape(N1, LANES) for h in range(2)]
        return jnp.concatenate(halves, axis=1)

    def dot(a, b, contract):
        return lax.dot_general(
            a, b, (((1,), (contract,)), ((), ())), preferred_element_type=jnp.float32
        )

    table_hi, table_lo = hi_ref[...], lo_ref[...]
    field_hi, field_lo = split_bf16(jnp.concatenate([part(0), part(1)], axis=0))
    first = dot(table_hi, field_hi, 0) + (
        dot(table_hi, field_lo, 0) + dot(table_lo, field_hi, 0)
    )
    re, im = first[:N1], first[N1:]
    turn_re, turn_im = turn_ref[0], turn_ref[1]
    turned = jnp.concatenate(
        [re * turn_re - im * turn_im, re * turn_im + im * turn_re], axis=1
    )
    turned_hi, turned_lo = split_bf16(turned)
    final = dot(table_hi, turned_hi, 1) + (
        dot(table_hi, turned_lo, 1) + dot(table_lo, turned_hi, 1)
    )
    for c in range(2):
        for h in range(2):
            out_ref[:, c, h] = final[
                c * N1 : (c + 1) * N1, h * LANES : (h + 1) * LANES
            ].reshape(ROWS, 8, LANES)


def tilt_kernel(base_ref, taps_ref, low_ref, own_ref, high_ref, jac_ref, phase_ref, out_ref, ext, total, sems):
    copies = [
        pltpu.make_async_copy(low_ref, ext.at[0:HALO], sems.at[0]),
        pltpu.make_async_copy(own_ref, ext.at[HALO : HALO + ROWS], sems.at[1]),
        pltpu.make_async_copy(high_ref, ext.at[HALO + ROWS :], sems.at[2]),
    ]
    for copy in copies:
        copy.start()
    for copy in copies:
        copy.wait()
    for r in range(ROWS):
        base = base_ref[r]
        acc = taps_ref[r, 0] * ext[base]
        for j in range(1, 4):
            acc = acc + taps_ref[r, j] * ext[base + j]
        total[r * SLAB : (r + 1) * SLAB, :] = acc
    for tile in range(TILES):
        start = (tile % 2) * 8 + tile // 2
        columns = slice(tile * LANES, (tile + 1) * LANES)
        re = total[pl.ds(start, ROWS, stride=SLAB), :]
        im = total[pl.ds(16 + start, ROWS, stride=SLAB), :]
        sine, cosine = sine_cosine(phase_ref[:, columns])
        jac = jac_ref[:, columns]
        out_ref[0, :, columns] = jac * (re * cosine - im * sine)
        out_ref[1, :, columns] = jac * (re * sine + im * cosine)


def neighbours(value):
    size = lax.axis_size("row")
    up = [(i, i + 1) for i in range(size - 1)]
    down = [(i + 1, i) for i in range(size - 1)]
    low = lax.ppermute(value[ROWS - HALO :], "row", up)
    high = lax.ppermute(value[:HALO], "row", down)
    return low, high


def shards(band, sources, taps, jacobian, phase):
    hi, lo, turn = dft_tables()
    f32 = jnp.float32
    slabs = pl.pallas_call(
        slab_kernel,
        out_shape=jax.ShapeDtypeStruct((ROWS * SLAB, LANES), f32),
        name="slabs",
    )(band)
    rows = lax.all_to_all(
        slabs.reshape(ROWS, 2, 2, 8, LANES), "col", split_axis=0, concat_axis=0, tiled=True
    )
    spectra = pl.pallas_call(
        transform_kernel,
        out_shape=jax.ShapeDtypeStruct((ROWS, 2, 2, 8, LANES), f32),
        name="transform",
        compiler_params=pltpu.CompilerParams(vmem_limit_bytes=24 * 2**20),
    )(rows, jnp.asarray(hi), jnp.asarray(lo), jnp.asarray(turn))
    own = lax.all_to_all(spectra, "col", split_axis=0, concat_axis=0, tiled=True)
    own = own.reshape(ROWS, SLAB, LANES)
    low, high = neighbours(own)
    base = sources[:, 0] - lax.axis_index("row") * ROWS + HALO
    vmem = pl.BlockSpec(memory_space=pltpu.VMEM)
    smem = pl.BlockSpec(memory_space=pltpu.SMEM)
    anywhere = pl.BlockSpec(memory_space=pl.ANY)
    return pl.pallas_call(
        tilt_kernel,
        out_shape=jax.ShapeDtypeStruct(band.shape, f32),
        in_specs=[smem, smem, anywhere, anywhere, anywhere, vmem, vmem],
        out_specs=vmem,
        scratch_shapes=[
            pltpu.VMEM((ROWS + 2 * HALO, SLAB, LANES), f32),
            pltpu.VMEM((ROWS * SLAB, LANES), f32),
            pltpu.SemaphoreType.DMA((3,)),
        ],
        name="tilt",
        compiler_params=pltpu.CompilerParams(vmem_limit_bytes=24 * 2**20),
    )(base, taps, low, own, high, jacobian, phase)


def solution(mesh):
    placed = (
        P(None, "row", "col"),
        P("row", None),
        P("row", None),
        P("row", "col"),
        P("row", "col"),
    )
    return jax.shard_map(
        shards, mesh=mesh, in_specs=placed, out_specs=P(None, "row", "col"), check_vma=False
    )
```

time: 476 us -> 57.7 us (0.12)
  other arithmetic: 303 us -> 0.68 us
  local copies, waits for them, and re-layouts: 125 us -> 0.82 us
  blocking collectives: 0 us -> 33.7 us
  waiting for transfers between devices: 25.6 us -> 8.37 us
  starting transfers between devices: 18.6 us -> 7.09 us
  Pallas kernels: 0 us -> 6.63 us
    unnamed x1 -> x0, other arithmetic: 291 us -> none
    unnamed x8 -> x13, local copies, waits for them, and re-layouts: 84.3 us -> 0.78 us
    all_to_all x0 -> x2, blocking collectives: none -> 33.7 us  [the longest x1 18.6 us: shards(): lax.all_to_all(slabs.reshape(ROWS, 2, 2, 8, LANES), 'col', split_axis=0,...]
    reshape x1 -> x0, local copies, waits for them, and re-layouts: 17.6 us -> none  [transform_band(): return result.reshape(2, rows_here, cols_here)]
    transpose x1 -> x0, local copies, waits for them, and re-layouts: 16.6 us -> none  [transform_rows(): return final.reshape(piece.shape)]
    all_to_all x2 -> x0, waiting for transfers between devices: 15.8 us -> none  [the longest x1 9.55 us: transform_band(): lax.all_to_all(spectra, 'col', split_axis=3, concat_axis=2, tiled=True)]
    all_to_all x2 -> x0, starting transfers between devices: 11.4 us -> none  [the longest x1 7.32 us: transform_band(): lax.all_to_all(blocks, 'col', split_axis=2, concat_axis=3, tiled=True)]
    pallas_call x0 -> x3, Pallas kernels: none -> 6.63 us  [the longest x1 2.38 us: shards(): pl.pallas_call(slab_kernel, out_shape=jax.ShapeDtypeStruct((ROWS * SLAB,...]
  transfers between devices with their start and end apart: 4 -> 2, of which waited for: 4 -> 2; matrix products, arithmetic and copies ran while one was open for 1% -> 1% of each run, Pallas kernels for 0% -> 0%
where the time goes in v1:
time: 57.7 us; the launch traced here: 57.3 us
  blocking collectives  33.7 us (58%)
  waiting for transfers between devices  8.37 us (15%)
  starting transfers between devices  7.09 us (12%)
  Pallas kernels  6.63 us (11%)
  local copies, waits for them, and re-layouts  0.82 us (1%)
  other arithmetic  0.68 us (1%)
    all_to_all x1, blocking collectives, shards(): lax.all_to_all(slabs.reshape(ROWS, 2, 2, 8, LANES), 'col', split_axis=0,...  18.6 us
    all_to_all x1, blocking collectives, shards(): lax.all_to_all(spectra, 'col', split_axis=0, concat_axis=0, tiled=True)  15 us
    ppermute x1, waiting for transfers between devices, neighbours(): high = lax.ppermute(value[:HALO], 'row', down)  5.34 us
    ppermute x1, starting transfers between devices, neighbours(): low = lax.ppermute(value[ROWS - HALO:], 'row', up)  5.17 us
    ppermute x1, waiting for transfers between devices, neighbours(): low = lax.ppermute(value[ROWS - HALO:], 'row', up)  3.03 us
    pallas_call x1, Pallas kernels, shards(): pl.pallas_call(slab_kernel, out_shape=jax.ShapeDtypeStruct((ROWS * SLAB,...  2.38 us
    pallas_call x1, Pallas kernels, shards(): pl.pallas_call(tilt_kernel, out_shape=jax.ShapeDtypeStruct(band.shape, f3...  2.36 us
    ppermute x1, starting transfers between devices, neighbours(): high = lax.ppermute(value[:HALO], 'row', down)  1.92 us
  transfers between devices with their start and end apart: 2, of which 2 were waited for; matrix products, arithmetic and copies ran while one was open for 1% of the time, Pallas kernels for 0%

profile of v1, /device:TPU:96, one launch (start us, length us, event | category | flops | bytes accessed | tf_op | source)
XLA Modules:
  0.0 57.3 jit_solution(17530875424997722270)
XLA Ops:
  0.0 0.0 copy-start.2
  0.0 2.4 %slabs.1 = f32[1024,128]{1,0:T(8,128)} custom-call(f32[2,32,2048]{2,1,0:T(8,128)} %band_ref.1), custom_call_target="tpu_custom_call" | custom-call | tf_op jit(solution)/shard_map/slabs/pallas_call | solution.py:145
  2.4 0.0 copy-start
  2.4 0.0 copy-start.1
  2.4 18.6 %all_to_all.10.in_ref = f32[32,2,2,8,128]{4,3,2,1,0:T(8,128)S(1)} all-to-all(f32[32,2,2,8,128]{4,3,2,1,0:T(8,128)} %bitcast.7), channel_id=1, replica_groups=mesh['row'=16,'col'=32] {'col'}, dimensions={0} | all-to-all | bytes 1048576 | tf_op jit(solution)/shard_map/all_to_all | solution.py:150
  21.0 0.0 copy-done.2
  21.0 0.0 copy-done
  21.0 0.0 copy-done.1
  21.0 1.9 %transform.1 = f32[32,2,2,8,128]{4,3,2,1,0:T(8,128)S(1)} custom-call(f32[32,2,2,8,128]{4,3,2,1,0:T(8,128)S(1)} %all_to_all.10.in_ref, bf16[512,512]{1,0:T(8,128)(2,1)S(1)} %copy-done.2, bf16[512,512]{1,0:T(8,128)(2,1)S(1)} %copy-done.1, f32[2,256,256]{2,1,0:T(8,128)S(1)} %copy-done), custom_call_target="tpu_custom_call" | custom-call | tf_op jit(solution)/shard_map/transform/pallas_call | solution.py:153
  22.9 15.0 %all_to_all.11 = f32[32,2,2,8,128]{4,3,2,1,0:T(8,128)S(1)} all-to-all(f32[32,2,2,8,128]{4,3,2,1,0:T(8,128)S(1)} %transform.1), channel_id=1, replica_groups=mesh['row'=16,'col'=32] {'col'}, dimensions={0} | all-to-all | bytes 1048576 | tf_op jit(solution)/shard_map/all_to_all | solution.py:159
  38.0 0.0 copy-start.3
  38.0 0.0 copy-start.4
  38.0 5.2 %collective-permute-start = (f32[16,32,128]{2,1,0:T(8,128)S(1)}, f32[16,32,128]{2,1,0:T(8,128)S(1)}, u32[]{:S(2)}, u32[]{:S(2)}) collective-permute-start(f32[16,32,128]{2,1,0:T(8,128)S(1)} %bitcast.9), channel_id=1, source_target_pairs={{0,32},{32,64},{64,96},{96,128},{128,160},{160,192},{192,224},{224... | collective-permute-start | bytes 786440 | tf_op jit(solution)/shard_map/ppermute | solution.py:137
  43.2 1.9 %collective-permute-start.1 = (f32[16,32,128]{2,1,0:T(8,128)S(1)}, f32[16,32,128]{2,1,0:T(8,128)S(1)}, u32[]{:S(2)}, u32[]{:S(2)}) collective-permute-start(f32[16,32,128]{2,1,0:T(8,128)S(1)} %bitcast.8), channel_id=1, source_target_pairs={{32,0},{64,32},{96,64},{128,96},{160,128},{192,160},{224,192},{256... | collective-permute-start | bytes 786440 | tf_op jit(solution)/shard_map/ppermute | solution.py:138
  45.1 0.0 copy-start.5
  45.1 0.7 %copy-done.5 = f32[32,4]{0,1:T(4,128)S(1)} copy-done((f32[32,4]{0,1:T(4,128)S(1)}, f32[32,4]{0,1:T(4,128)}, u32[]{:S(2)}) %copy-start.5) | copy-done | bytes 536
  45.8 0.1 copy.9.taps_ref
  45.9 0.7 %add_bitcast_fusion.base_ref = s32[32]{0:T(128)S(1)} fusion(s32[32,4]{0,1:T(4,128)} %param.9, s32[]{:T(128)S(6)} %mul.3), kind=kLoop, calls=%fused_computation | loop fusion | flops 64 | bytes 260 | tf_op jit(solution)/shard_map/add | solution.py:162
  46.6 3.0 %collective-permute-done.low_ref = f32[16,32,128]{2,1,0:T(8,128)S(1)} collective-permute-done((f32[16,32,128]{2,1,0:T(8,128)S(1)}, f32[16,32,128]{2,1,0:T(8,128)S(1)}, u32[]{:S(2)}, u32[]{:S(2)}) %collective-permute-start) | collective-permute-done | bytes 262176 | tf_op jit(solution)/shard_map/ppermute | solution.py:137
  49.6 5.3 %collective-permute-done.1.high_ref = f32[16,32,128]{2,1,0:T(8,128)S(1)} collective-permute-done((f32[16,32,128]{2,1,0:T(8,128)S(1)}, f32[16,32,128]{2,1,0:T(8,128)S(1)}, u32[]{:S(2)}, u32[]{:S(2)}) %collective-permute-start.1) | collective-permute-done | bytes 262176 | tf_op jit(solution)/shard_map/ppermute | solution.py:138
  55.0 0.0 copy-done.3
  55.0 0.0 copy-done.4
  55.0 2.4 %tilt.1 = f32[2,32,2048]{2,1,0:T(8,128)} custom-call(s32[32]{0:T(128)S(1)} %add_bitcast_fusion.base_ref, f32[32,4]{1,0:T(8,128)S(1)} %copy.9.taps_ref, f32[16,32,128]{2,1,0:T(8,128)S(1)} %collective-permute-done.low_ref, f32[32,32,128]{2,1,0:T(8,128)S(1)} %bitcast.6, f32[16,32,128]{2,1,0:T(8,128)S(1)} %collective-permute-done.1.high_ref, ...), custom_call_target="tpu_custom_call" | custom-call | tf_op jit(solution)/shard_map/tilt/pallas_call | solution.py:166
  (1 shorter events, 0.0 us)
Async XLA Ops:
  0.0 21.0 %copy-start.2 = (bf16[512,512]{1,0:T(8,128)(2,1)S(1)}, bf16[512,512]{1,0:T(8,128)(2,1)}, u32[]{:S(2)}) copy-start(bf16[512,512]{1,0:T(8,128)(2,1)} %constant.16.clone.hi_ref) | copy-start | bytes 1572868
  2.4 18.6 %copy-start = (f32[2,256,256]{2,1,0:T(8,128)S(1)}, f32[2,256,256]{2,1,0:T(8,128)}, u32[]{:S(2)}) copy-start(f32[2,256,256]{2,1,0:T(8,128)} %constant.18.clone.turn_ref) | copy-start | bytes 1572868
  2.4 18.6 %copy-start.1 = (bf16[512,512]{1,0:T(8,128)(2,1)S(1)}, bf16[512,512]{1,0:T(8,128)(2,1)}, u32[]{:S(2)}) copy-start(bf16[512,512]{1,0:T(8,128)(2,1)} %constant.17.clone.lo_ref) | copy-start | bytes 1572868
  38.0 17.0 %copy-start.3 = (f32[32,2048]{1,0:T(8,128)S(1)}, f32[32,2048]{1,0:T(8,128)}, u32[]{:S(2)}) copy-start(f32[32,2048]{1,0:T(8,128)} %jac_ref.1) | copy-start | bytes 786436
  38.0 17.0 %copy-start.4 = (f32[32,2048]{1,0:T(8,128)S(1)}, f32[32,2048]{1,0:T(8,128)}, u32[]{:S(2)}) copy-start(f32[32,2048]{1,0:T(8,128)} %phase_ref.1) | copy-start | bytes 786436
  38.0 11.6 %collective-permute-start = (f32[16,32,128]{2,1,0:T(8,128)S(1)}, f32[16,32,128]{2,1,0:T(8,128)S(1)}, u32[]{:S(2)}, u32[]{:S(2)}) collective-permute-start(f32[16,32,128]{2,1,0:T(8,128)S(1)} %bitcast.9), channel_id=1, source_target_pairs={{0,32},{32,64},{64,96},{96,128},{128,160},{160,192},{192,224},{224... | collective-permute-start | bytes 786440 | tf_op jit(solution)/shard_map/ppermute | solution.py:137
  43.2 11.8 %collective-permute-start.1 = (f32[16,32,128]{2,1,0:T(8,128)S(1)}, f32[16,32,128]{2,1,0:T(8,128)S(1)}, u32[]{:S(2)}, u32[]{:S(2)}) collective-permute-start(f32[16,32,128]{2,1,0:T(8,128)S(1)} %bitcast.8), channel_id=1, source_target_pairs={{32,0},{64,32},{96,64},{128,96},{160,128},{192,160},{224,192},{256... | collective-permute-start | bytes 786440 | tf_op jit(solution)/shard_map/ppermute | solution.py:138
  45.1 0.7 %copy-start.5 = (f32[32,4]{0,1:T(4,128)S(1)}, f32[32,4]{0,1:T(4,128)}, u32[]{:S(2)}) copy-start(f32[32,4]{0,1:T(4,128)} %param.10) | copy-start | bytes 1540

commit v2 on v1

v2 whole, which is shorter than its diff:
```python
import math

import jax
import jax.numpy as jnp
import numpy as np
from jax import lax
from jax.experimental import pallas as pl
from jax.experimental.pallas import tpu as pltpu
from jax.sharding import PartitionSpec as P

N1 = 256
LANES = 128
ROWS = 32
HALO = 16
TILES = 16
GROUPS = 4
SLAB = 32


def split_bf16(x):
    hi = x.astype(jnp.bfloat16)
    lo = (x - hi.astype(jnp.float32)).astype(jnp.bfloat16)
    return hi, lo


def dft_tables():
    idx = np.arange(N1, dtype=np.int64)
    ang = 2.0 * np.pi * ((idx[:, None] * idx[None, :]) % N1) / N1
    table = np.concatenate([np.cos(ang), np.sin(ang)], axis=1)
    hi = table.astype(np.float32).astype(jnp.bfloat16)
    lo = (table - hi.astype(np.float64)).astype(np.float32).astype(jnp.bfloat16)
    twist = -2.0 * np.pi * (idx[:, None] * idx[None, :]) / (N1 * N1)
    scale = 1.0 / N1
    turn = np.stack([np.cos(twist) * scale, np.sin(twist) * scale]).astype(np.float32)
    return hi, lo, turn


def sine_cosine_coefficients():
    nodes = np.cos((np.arange(400) + 0.5) * np.pi / 400) * (np.pi / 2)
    square = nodes * nodes
    sinc = np.where(nodes == 0, 1.0, np.sin(nodes) / nodes)
    powers = np.stack([square**i for i in range(7)], axis=1)
    sine = np.linalg.lstsq(powers, sinc, rcond=None)[0]
    cosine = np.linalg.lstsq(powers, np.cos(nodes), rcond=None)[0]
    return [float(v) for v in sine], [float(v) for v in cosine]


SINE, COSINE = sine_cosine_coefficients()


def polynomial(square, coefficients):
    total = jnp.full_like(square, coefficients[-1])
    for value in coefficients[-2::-1]:
        total = total * square + value
    return total


def sine_cosine(x):
    half = 0.5 * x
    square = half * half
    s = half * polynomial(square, SINE)
    c = polynomial(square, COSINE)
    return 2.0 * s * c, 1.0 - 2.0 * s * s


def tile_start(tile):
    return (tile % 2) * 8 + tile // 2


def slab_kernel(band_ref, out_ref):
    for group in range(GROUPS):
        rows = slice(8 * group, 8 * group + 8)
        for c in range(2):
            for tile in range(TILES):
                start = 8 * group * SLAB + c * 16 + tile_start(tile)
                out_ref[pl.ds(start, 8, stride=SLAB), :] = band_ref[
                    c, rows, tile * LANES : (tile + 1) * LANES
                ]


def transform_kernel(in_ref, hi_ref, lo_ref, turn_ref, out_ref):
    def part(c):
        halves = [in_ref[:, c, h].reshape(N1, LANES) for h in range(2)]
        return jnp.concatenate(halves, axis=1)

    def blocks(re, im):
        upper = jnp.concatenate([re, im], axis=1)
        return jnp.concatenate([upper, jnp.concatenate([im, -re], axis=1)], axis=0)

    def stage(re, im, contract):
        def dot(a, b):
            return lax.dot_general(
                a, b, (((1,), (contract,)), ((), ())), preferred_element_type=jnp.float32
            )

        re_hi, re_lo = split_bf16(re)
        im_hi, im_lo = split_bf16(im)
        hi, lo = blocks(re_hi, im_hi), blocks(re_lo, im_lo)
        return dot(hi_ref[...], hi) + (dot(hi_ref[...], lo) + dot(lo_ref[...], hi))

    first = stage(part(0), part(1), 0)
    re, im = first[:, :N1], first[:, N1:]
    turn_re, turn_im = turn_ref[0], turn_ref[1]
    final = stage(re * turn_re - im * turn_im, re * turn_im + im * turn_re, 1)
    for c in range(2):
        for h in range(2):
            start = c * N1 + h * LANES
            out_ref[:, c, h] = final[:, start : start + LANES].reshape(ROWS, 8, LANES)


def core_parity():
    return lax.axis_index("col") % 2


def border_kernel(own_ref, first_ref, second_ref):
    def put(last_ref, initial_ref):
        last_ref[...] = own_ref[ROWS - HALO :]
        initial_ref[...] = own_ref[:HALO]

    parity = core_parity()
    pl.when(parity == 0)(lambda: put(first_ref, second_ref))
    pl.when(parity == 1)(lambda: put(second_ref, first_ref))


def turn_kernel(sources_ref, taps_ref, jac_ref, phase_ref, own_ref, cos_ref, sin_ref, base_ref, weight_ref):
    for tile in range(TILES):
        columns = slice(tile * LANES, (tile + 1) * LANES)
        sine, cosine = sine_cosine(phase_ref[:, columns])
        jac = jac_ref[:, columns]
        cos_ref[:, columns] = jac * cosine
        sin_ref[:, columns] = jac * sine
    shift = HALO - lax.axis_index("row") * ROWS
    for r in range(ROWS):
        base_ref[r : r + 1, :] = jnp.full((1, LANES), sources_ref[0, r] + shift, jnp.int32)
        for j in range(4):
            weight_ref[4 * r + j : 4 * r + j + 1, :] = jnp.full(
                (1, LANES), taps_ref[j, r], jnp.float32
            )


def tilt_kernel(base_ref, weight_ref, own_ref, first_ref, second_ref, cos_ref, sin_ref, out_ref, ext, total, held, sems):
    def put(low_ref, high_ref):
        ext[:HALO] = low_ref[...]
        ext[HALO + ROWS :] = high_ref[...]

    parity = core_parity()
    pl.when(parity == 0)(lambda: put(first_ref, second_ref))
    pl.when(parity == 1)(lambda: put(second_ref, first_ref))
    ext[HALO : HALO + ROWS] = own_ref[...]
    copies = []
    for group in range(GROUPS):
        for r in range(8 * group, 8 * group + 8):
            base = base_ref[r : r + 1, 0:1][0, 0]
            acc = weight_ref[4 * r : 4 * r + 1, :] * ext[base]
            for j in range(1, 4):
                acc = acc + weight_ref[4 * r + j : 4 * r + j + 1, :] * ext[base + j]
            total[r * SLAB : (r + 1) * SLAB, :] = acc
        rows = slice(8 * group, 8 * group + 8)
        for tile in range(TILES):
            columns = slice(tile * LANES, (tile + 1) * LANES)
            start = 8 * group * SLAB + tile_start(tile)
            re = total[pl.ds(start, 8, stride=SLAB), :]
            im = total[pl.ds(16 + start, 8, stride=SLAB), :]
            cosine, sine = cos_ref[rows, columns], sin_ref[rows, columns]
            held[group, 0, :, columns] = re * cosine - im * sine
            held[group, 1, :, columns] = re * sine + im * cosine
        copies.append(
            pltpu.make_async_copy(held.at[group], out_ref.at[:, rows], sems.at[group])
        )
        copies[-1].start()
    for copy in copies:
        copy.wait()


def plane_shift(value, even_step):
    planes, columns = lax.axis_size("row"), lax.axis_size("col")
    pairs = []
    for g in range(planes):
        for c in range(columns):
            to = g + (even_step if c % 2 == 0 else -even_step)
            if 0 <= to < planes:
                pairs.append((g * columns + c, to * columns + c))
    return lax.ppermute(value, ("row", "col"), pairs)


def shards(band, sources, taps, jacobian, phase):
    hi, lo, turn = dft_tables()
    f32 = jnp.float32
    vmem = pl.BlockSpec(memory_space=pltpu.VMEM)
    smem = pl.BlockSpec(memory_space=pltpu.SMEM)
    hbm = pl.BlockSpec(memory_space=pltpu.HBM)
    limit = pltpu.CompilerParams(vmem_limit_bytes=16 * 2**20)
    slabs = pl.pallas_call(
        slab_kernel,
        out_shape=jax.ShapeDtypeStruct((ROWS * SLAB, LANES), f32),
        name="slabs",
        compiler_params=limit,
    )(band)
    rows = lax.all_to_all(
        slabs.reshape(ROWS, 2, 2, 8, LANES), "col", split_axis=0, concat_axis=0, tiled=True
    )
    spectra = pl.pallas_call(
        transform_kernel,
        out_shape=jax.ShapeDtypeStruct((ROWS, 2, 2, 8, LANES), f32),
        name="transform",
        compiler_params=limit,
    )(rows, jnp.asarray(hi), jnp.asarray(lo), jnp.asarray(turn))
    own = lax.all_to_all(spectra, "col", split_axis=0, concat_axis=0, tiled=True)
    own = own.reshape(ROWS, SLAB, LANES)
    border = jax.ShapeDtypeStruct((HALO, SLAB, LANES), f32)
    first, second = pl.pallas_call(
        border_kernel, out_shape=[border, border], name="border_rows", compiler_params=limit
    )(own)
    first = plane_shift(first, 1)
    second = plane_shift(second, -1)
    weights = jax.ShapeDtypeStruct(jacobian.shape, f32)
    cosine, sine, base, weight = pl.pallas_call(
        turn_kernel,
        out_shape=[
            weights,
            weights,
            jax.ShapeDtypeStruct((ROWS, LANES), jnp.int32),
            jax.ShapeDtypeStruct((4 * ROWS, LANES), f32),
        ],
        in_specs=[smem, smem, vmem, vmem, pl.BlockSpec(memory_space=pl.ANY)],
        name="turn",
        compiler_params=limit,
    )(sources.T, taps.T, jacobian, phase, own)
    return pl.pallas_call(
        tilt_kernel,
        out_shape=jax.ShapeDtypeStruct(band.shape, f32),
        in_specs=[vmem] * 7,
        out_specs=hbm,
        scratch_shapes=[
            pltpu.VMEM((ROWS + 2 * HALO, SLAB, LANES), f32),
            pltpu.VMEM((ROWS * SLAB, LANES), f32),
            pltpu.VMEM((GROUPS, 2, 8, TILES * LANES), f32),
            pltpu.SemaphoreType.DMA((GROUPS,)),
        ],
        name="tilt",
        compiler_params=limit,
    )(base, weight, own, first, second, cosine, sine)


def solution(mesh):
    placed = (
        P(None, "row", "col"),
        P("row", None),
        P("row", None),
        P("row", "col"),
        P("row", "col"),
    )
    return jax.shard_map(
        shards, mesh=mesh, in_specs=placed, out_specs=P(None, "row", "col"), check_vma=False
    )
```

time: 57.7 us -> 52.2 us (0.905)
  Pallas kernels: 6.63 us -> 3.64 us
  waiting for transfers between devices: 8.37 us -> 6.55 us
  other arithmetic: 0.68 us -> 0 us
    pallas_call x1, Pallas kernels: 2.38 us -> 0.31 us  [shards(): pl.pallas_call(slab_kernel, out_shape=jax.ShapeDtypeStruct((ROWS * SLAB,...]
    ppermute x2, waiting for transfers between devices: 8.37 us -> 6.55 us  [plane_shift(): return lax.ppermute(value, ('row', 'col'), pairs)]
    pallas_call x1, Pallas kernels: 2.36 us -> 1.24 us  [shards(): pl.pallas_call(tilt_kernel, out_shape=jax.ShapeDtypeStruct(band.shape, f3...]
    pallas_call x0 -> x2, Pallas kernels: none -> 0.98 us  [the longest x1 0.95 us: shards(): pl.pallas_call(turn_kernel, out_shape=[weights, weights, jax.ShapeDtypeSt...]
    pallas_call x1, Pallas kernels: 1.9 us -> 1.12 us  [shards(): pl.pallas_call(transform_kernel, out_shape=jax.ShapeDtypeStruct((ROWS, 2,...]
    add x1 -> x0, other arithmetic: 0.68 us -> none  [shards(): base = sources[:, 0] - lax.axis_index('row') * ROWS + HALO]
  transfers between devices with their start and end apart: 2 -> 2, of which waited for: 2 -> 2; matrix products, arithmetic and copies ran while one was open for 1% -> 0% of each run, Pallas kernels for 0% -> 2%
where the time goes in v2:
time: 52.2 us; the launch traced here: 52 us
  blocking collectives  33.5 us (64%)
  starting transfers between devices  7.08 us (14%)
  waiting for transfers between devices  6.55 us (13%)
  Pallas kernels  3.64 us (7%)
  local copies, waits for them, and re-layouts  1.08 us (2%)
    all_to_all x1, blocking collectives, shards(): lax.all_to_all(slabs.reshape(ROWS, 2, 2, 8, LANES), 'col', split_axis=0,...  18.4 us
    all_to_all x1, blocking collectives, shards(): lax.all_to_all(spectra, 'col', split_axis=0, concat_axis=0, tiled=True)  15.1 us
    ppermute x2, starting transfers between devices, plane_shift(): return lax.ppermute(value, ('row', 'col'), pairs)  7.08 us
    ppermute x2, waiting for transfers between devices, plane_shift(): return lax.ppermute(value, ('row', 'col'), pairs)  6.55 us
    pallas_call x1, Pallas kernels, shards(): pl.pallas_call(tilt_kernel, out_shape=jax.ShapeDtypeStruct(band.shape, f3...  1.24 us
    pallas_call x1, Pallas kernels, shards(): pl.pallas_call(transform_kernel, out_shape=jax.ShapeDtypeStruct((ROWS, 2,...  1.12 us
    unnamed x16, local copies, waits for them, and re-layouts  1.08 us
  transfers between devices with their start and end apart: 2, of which 2 were waited for; matrix products, arithmetic and copies ran while one was open for 0% of the time, Pallas kernels for 2%

profile of v2, /device:TPU:96, one launch (start us, length us, event | category | flops | bytes accessed | tf_op | source)
XLA Modules:
  0.0 52.0 jit_solution(782880169149010022)
XLA Ops:
  0.0 0.0 copy-start
  0.0 1.0 %copy-done = f32[2,32,2048]{2,1,0:T(8,128)S(1)} copy-done((f32[2,32,2048]{2,1,0:T(8,128)S(1)}, f32[2,32,2048]{2,1,0:T(8,128)}, u32[]{:S(2)}) %copy-start) | copy-done | bytes 524312
  1.0 0.3 slabs.1
  1.4 0.0 copy-start.1
  1.4 0.0 copy-start.4
  1.4 0.0 copy-start.5
  1.4 18.4 %all_to_all.10.in_ref = f32[32,2,2,8,128]{4,3,2,1,0:T(8,128)S(1)} all-to-all(f32[32,2,2,8,128]{4,3,2,1,0:T(8,128)S(1)} %bitcast.7), channel_id=1, replica_groups=mesh['row'=16,'col'=32] {'col'}, dimensions={0} | all-to-all | bytes 1048576 | tf_op jit(solution)/shard_map/all_to_all | solution.py:199
  19.8 0.0 copy-done.1
  19.8 0.0 copy-done.4
  19.8 0.0 copy-done.5
  19.8 1.1 %transform.1 = f32[32,2,2,8,128]{4,3,2,1,0:T(8,128)S(1)} custom-call(f32[32,2,2,8,128]{4,3,2,1,0:T(8,128)S(1)} %all_to_all.10.in_ref, bf16[256,512]{1,0:T(8,128)(2,1)S(1)} %copy-done.5, bf16[256,512]{1,0:T(8,128)(2,1)S(1)} %copy-done.4, f32[2,256,256]{2,1,0:T(8,128)S(1)} %copy-done.1), custom_call_target="tpu_custom_call" | custom-call | tf_op jit(solution)/shard_map/transform/pallas_call | solution.py:202
  21.0 15.1 %all_to_all.11 = f32[32,2,2,8,128]{4,3,2,1,0:T(8,128)S(1)} all-to-all(f32[32,2,2,8,128]{4,3,2,1,0:T(8,128)S(1)} %transform.1), channel_id=1, replica_groups=mesh['row'=16,'col'=32] {'col'}, dimensions={0} | all-to-all | bytes 1048576 | tf_op jit(solution)/shard_map/all_to_all | solution.py:208
  36.1 5.2 %collective-permute-start = (f32[16,32,128]{2,1,0:T(8,128)S(1)}, f32[16,32,128]{2,1,0:T(8,128)S(1)}, u32[]{:S(2)}, u32[]{:S(2)}) collective-permute-start(f32[16,32,128]{2,1,0:T(8,128)S(1)} %get-tuple-element.13), channel_id=1, source_target_pairs={{0,32},{2,34},{4,36},{6,38},{8,40},{10,42},{12,44},{14,46},{16,48}... | collective-permute-start | bytes 786440 | tf_op jit(solution)/shard_map/ppermute | solution.py:183
  41.2 0.0 copy-start.7
  41.3 0.0 copy-start.6
  41.3 1.9 %collective-permute-start.1 = (f32[16,32,128]{2,1,0:T(8,128)S(1)}, f32[16,32,128]{2,1,0:T(8,128)S(1)}, u32[]{:S(2)}, u32[]{:S(2)}) collective-permute-start(f32[16,32,128]{2,1,0:T(8,128)S(1)} %get-tuple-element.14), channel_id=1, source_target_pairs={{1,33},{3,35},{5,37},{7,39},{9,41},{11,43},{13,45},{15,47},{17,49}... | collective-permute-start | bytes 786440 | tf_op jit(solution)/shard_map/ppermute | solution.py:183
  43.2 0.0 copy-done.2
  43.2 0.0 copy-done.3
  43.2 0.0 copy-done.7
  43.2 0.0 copy-done.6
  43.2 0.9 %turn.1 = (f32[32,2048]{1,0:T(8,128)S(1)}, f32[32,2048]{1,0:T(8,128)S(1)}, s32[32,128]{1,0:T(8,128)S(1)}, f32[128,128]{1,0:T(8,128)S(1)}) custom-call(s32[4,32]{1,0:T(4,128)S(1)} %bitcast.8, f32[4,32]{1,0:T(4,128)S(1)} %bitcast.9, f32[32,2048]{1,0:T(8,128)S(1)} %copy-done.2, f32[32,2048]{1,0:T(8,128)S(1)} %copy-done.3, f32[32,32,128]{2,1,0:T(8,128)S(1)} %bitcast.5), custom_call_target="tpu_custom_call" | custom-call | tf_op jit(solution)/shard_map/turn/pallas_call | solution.py:217
  44.2 2.0 %collective-permute-done.first_ref = f32[16,32,128]{2,1,0:T(8,128)S(1)} collective-permute-done((f32[16,32,128]{2,1,0:T(8,128)S(1)}, f32[16,32,128]{2,1,0:T(8,128)S(1)}, u32[]{:S(2)}, u32[]{:S(2)}) %collective-permute-start) | collective-permute-done | bytes 262176 | tf_op jit(solution)/shard_map/ppermute | solution.py:183
  46.2 4.6 %collective-permute-done.1.second_ref = f32[16,32,128]{2,1,0:T(8,128)S(1)} collective-permute-done((f32[16,32,128]{2,1,0:T(8,128)S(1)}, f32[16,32,128]{2,1,0:T(8,128)S(1)}, u32[]{:S(2)}, u32[]{:S(2)}) %collective-permute-start.1) | collective-permute-done | bytes 262176 | tf_op jit(solution)/shard_map/ppermute | solution.py:183
  50.7 1.2 %tilt.1 = f32[2,32,2048]{2,1,0:T(8,128)} custom-call(s32[32,128]{1,0:T(8,128)S(1)} %get-tuple-element.11.base_ref, f32[128,128]{1,0:T(8,128)S(1)} %get-tuple-element.12.weight_ref, f32[32,32,128]{2,1,0:T(8,128)S(1)} %bitcast.6, f32[16,32,128]{2,1,0:T(8,128)S(1)} %collective-permute-done.first_ref, f32[16,32,128]{2,1,0:T(8,128)S(1)} %collective-permute-done.1.second_ref, ...), custom_call_target="tpu_custom_call" | custom-call | tf_op jit(solution)/shard_map/tilt/pallas_call | solution.py:229
  (3 shorter events, 0.0 us)
Async XLA Ops:
  0.0 1.0 %copy-start = (f32[2,32,2048]{2,1,0:T(8,128)S(1)}, f32[2,32,2048]{2,1,0:T(8,128)}, u32[]{:S(2)}) copy-start(f32[2,32,2048]{2,1,0:T(8,128)} %band_ref.1) | copy-start | bytes 1572868
  1.4 18.5 %copy-start.1 = (f32[2,256,256]{2,1,0:T(8,128)S(1)}, f32[2,256,256]{2,1,0:T(8,128)}, u32[]{:S(2)}) copy-start(f32[2,256,256]{2,1,0:T(8,128)} %constant.8.clone.turn_ref) | copy-start | bytes 1572868
  1.4 18.5 %copy-start.4 = (bf16[256,512]{1,0:T(8,128)(2,1)S(1)}, bf16[256,512]{1,0:T(8,128)(2,1)}, u32[]{:S(2)}) copy-start(bf16[256,512]{1,0:T(8,128)(2,1)} %constant.7.clone.lo_ref) | copy-start | bytes 786436
  1.4 18.5 %copy-start.5 = (bf16[256,512]{1,0:T(8,128)(2,1)S(1)}, bf16[256,512]{1,0:T(8,128)(2,1)}, u32[]{:S(2)}) copy-start(bf16[256,512]{1,0:T(8,128)(2,1)} %constant.6.clone.hi_ref) | copy-start | bytes 786436
  36.0 7.2 %copy-start.2 = (f32[32,2048]{1,0:T(8,128)S(1)}, f32[32,2048]{1,0:T(8,128)}, u32[]{:S(2)}) copy-start(f32[32,2048]{1,0:T(8,128)} %jac_ref.1) | copy-start | bytes 786436
  36.0 7.2 %copy-start.3 = (f32[32,2048]{1,0:T(8,128)S(1)}, f32[32,2048]{1,0:T(8,128)}, u32[]{:S(2)}) copy-start(f32[32,2048]{1,0:T(8,128)} %phase_ref.1) | copy-start | bytes 786436
  36.1 10.1 %collective-permute-start = (f32[16,32,128]{2,1,0:T(8,128)S(1)}, f32[16,32,128]{2,1,0:T(8,128)S(1)}, u32[]{:S(2)}, u32[]{:S(2)}) collective-permute-start(f32[16,32,128]{2,1,0:T(8,128)S(1)} %get-tuple-element.13), channel_id=1, source_target_pairs={{0,32},{2,34},{4,36},{6,38},{8,40},{10,42},{12,44},{14,46},{16,48}... | collective-permute-start | bytes 786440 | tf_op jit(solution)/shard_map/ppermute | solution.py:183
  41.2 2.0 %copy-start.7 = (f32[32,4]{0,1:T(4,128)S(1)}, f32[32,4]{0,1:T(4,128)}, u32[]{:S(2)}) copy-start(f32[32,4]{0,1:T(4,128)} %param.10) | copy-start | bytes 1540
  41.3 2.0 %copy-start.6 = (s32[32,4]{0,1:T(4,128)S(1)}, s32[32,4]{0,1:T(4,128)}, u32[]{:S(2)}) copy-start(s32[32,4]{0,1:T(4,128)} %param.9) | copy-start | bytes 1540
  41.3 9.5 %collective-permute-start.1 = (f32[16,32,128]{2,1,0:T(8,128)S(1)}, f32[16,32,128]{2,1,0:T(8,128)S(1)}, u32[]{:S(2)}, u32[]{:S(2)}) collective-permute-start(f32[16,32,128]{2,1,0:T(8,128)S(1)} %get-tuple-element.14), channel_id=1, source_target_pairs={{1,33},{3,35},{5,37},{7,39},{9,41},{11,43},{13,45},{15,47},{17,49}... | collective-permute-start | bytes 786440 | tf_op jit(solution)/shard_map/ppermute | solution.py:183

commit v3 on v2

--- a/solution.py
+++ b/solution.py
@@ -13,6 +13,7 @@
 ROWS = 32
 HALO = 16
 TILES = 16
+HALF_GROUPS = 2
 GROUPS = 4
 SLAB = 32
 
@@ -67,14 +68,22 @@
     return (tile % 2) * 8 + tile // 2
 
 
-def slab_kernel(band_ref, out_ref):
+def slab_kernel(band_ref, out_ref, held, sems):
+    copies = [
+        pltpu.make_async_copy(
+            band_ref.at[:, 8 * group : 8 * group + 8], held.at[group], sems.at[group]
+        )
+        for group in range(GROUPS)
+    ]
+    for copy in copies:
+        copy.start()
     for group in range(GROUPS):
-        rows = slice(8 * group, 8 * group + 8)
+        copies[group].wait()
         for c in range(2):
             for tile in range(TILES):
                 start = 8 * group * SLAB + c * 16 + tile_start(tile)
-                out_ref[pl.ds(start, 8, stride=SLAB), :] = band_ref[
-                    c, rows, tile * LANES : (tile + 1) * LANES
+                out_ref[pl.ds(start, 8, stride=SLAB), :] = held[
+                    group, c, :, tile * LANES : (tile + 1) * LANES
                 ]
 
 
@@ -131,31 +140,37 @@
         sin_ref[:, columns] = jac * sine
     shift = HALO - lax.axis_index("row") * ROWS
     for r in range(ROWS):
-        base_ref[r : r + 1, :] = jnp.full((1, LANES), sources_ref[0, r] + shift, jnp.int32)
+        base_ref[r : r + 1, :] = jnp.full((1, LANES), sources_ref[0, r] + shift - (HALO if r >= HALO else 0), jnp.int32)
         for j in range(4):
             weight_ref[4 * r + j : 4 * r + j + 1, :] = jnp.full(
                 (1, LANES), taps_ref[j, r], jnp.float32
             )
 
 
-def tilt_kernel(base_ref, weight_ref, own_ref, first_ref, second_ref, cos_ref, sin_ref, out_ref, ext, total, held, sems):
-    def put(low_ref, high_ref):
-        ext[:HALO] = low_ref[...]
-        ext[HALO + ROWS :] = high_ref[...]
-
-    parity = core_parity()
-    pl.when(parity == 0)(lambda: put(first_ref, second_ref))
-    pl.when(parity == 1)(lambda: put(second_ref, first_ref))
-    ext[HALO : HALO + ROWS] = own_ref[...]
+def tilt_half(late, base_ref, weight_ref, own_ref, halo_ref, cos_ref, sin_ref, out_ref, ext, total, held, sems):
+    half = (core_parity() + late) % 2
+
+    @pl.when(half == 0)
+    def _():
+        ext[:HALO] = halo_ref[...]
+        ext[HALO:] = own_ref[...]
+
+    @pl.when(half == 1)
+    def _():
+        ext[:ROWS] = own_ref[...]
+        ext[ROWS:] = halo_ref[...]
+
+    offset = pl.multiple_of(half * HALO, HALO)
     copies = []
-    for group in range(GROUPS):
+    for group in range(HALF_GROUPS):
         for r in range(8 * group, 8 * group + 8):
-            base = base_ref[r : r + 1, 0:1][0, 0]
-            acc = weight_ref[4 * r : 4 * r + 1, :] * ext[base]
+            base = base_ref[pl.ds(offset + r, 1), 0:1][0, 0]
+            weights = weight_ref[pl.ds(pl.multiple_of(4 * offset, 4 * HALO) + 4 * r, 4), :]
+            acc = weights[0:1] * ext[base]
             for j in range(1, 4):
-                acc = acc + weight_ref[4 * r + j : 4 * r + j + 1, :] * ext[base + j]
+                acc = acc + weights[j : j + 1] * ext[base + j]
             total[r * SLAB : (r + 1) * SLAB, :] = acc
-        rows = slice(8 * group, 8 * group + 8)
+        rows = pl.ds(pl.multiple_of(offset + 8 * group, 8), 8)
         for tile in range(TILES):
             columns = slice(tile * LANES, (tile + 1) * LANES)
             start = 8 * group * SLAB + tile_start(tile)
@@ -172,6 +187,14 @@
         copy.wait()
 
 
+def early_kernel(*refs):
+    tilt_half(0, *refs)
+
+
+def late_kernel(early_ref, *refs):
+    tilt_half(1, *refs)
+
+
 def plane_shift(value, even_step):
     planes, columns = lax.axis_size("row"), lax.axis_size("col")
     pairs = []
@@ -193,8 +216,13 @@
     slabs = pl.pallas_call(
         slab_kernel,
         out_shape=jax.ShapeDtypeStruct((ROWS * SLAB, LANES), f32),
+        in_specs=[pl.BlockSpec(memory_space=pl.ANY)],
+        scratch_shapes=[
+            pltpu.VMEM((GROUPS, 2, 8, TILES * LANES), f32),
+            pltpu.SemaphoreType.DMA((GROUPS,)),
+        ],
         name="slabs",
-        compiler_params=limit,
+        compiler_params=pltpu.CompilerParams(vmem_limit_bytes=56000000),
     )(band)
     rows = lax.all_to_all(
         slabs.reshape(ROWS, 2, 2, 8, LANES), "col", split_axis=0, concat_axis=0, tiled=True
@@ -226,20 +254,32 @@
         name="turn",
         compiler_params=limit,
     )(sources.T, taps.T, jacobian, phase, own)
+    any_space = pl.BlockSpec(memory_space=pl.ANY)
+    scratch = [
+        pltpu.VMEM((ROWS + HALO, SLAB, LANES), f32),
+        pltpu.VMEM((HALO * SLAB, LANES), f32),
+        pltpu.VMEM((HALF_GROUPS, 2, 8, TILES * LANES), f32),
+        pltpu.SemaphoreType.DMA((HALF_GROUPS,)),
+    ]
+    early = pl.pallas_call(
+        early_kernel,
+        out_shape=jax.ShapeDtypeStruct(band.shape, f32),
+        in_specs=[vmem] * 6,
+        out_specs=hbm,
+        scratch_shapes=scratch,
+        name="tilt_early",
+        compiler_params=limit,
+    )(base, weight, own, first, cosine, sine)
     return pl.pallas_call(
-        tilt_kernel,
+        late_kernel,
         out_shape=jax.ShapeDtypeStruct(band.shape, f32),
-        in_specs=[vmem] * 7,
+        in_specs=[any_space] + [vmem] * 6,
         out_specs=hbm,
-        scratch_shapes=[
-            pltpu.VMEM((ROWS + 2 * HALO, SLAB, LANES), f32),
-            pltpu.VMEM((ROWS * SLAB, LANES), f32),
-            pltpu.VMEM((GROUPS, 2, 8, TILES * LANES), f32),
-            pltpu.SemaphoreType.DMA((GROUPS,)),
-        ],
-        name="tilt",
-        compiler_params=limit,
-    )(base, weight, own, first, second, cosine, sine)
+        input_output_aliases={0: 0},
+        scratch_shapes=scratch,
+        name="tilt_late",
+        compiler_params=limit,
+    )(early, base, weight, own, second, cosine, sine)
 
 
 def solution(mesh):

time: 52.2 us -> 51.9 us (level)
  Pallas kernels: 3.64 us -> 5.36 us
  local copies, waits for them, and re-layouts: 1.08 us -> 0.04 us
  waiting for transfers between devices: 6.55 us -> 5.54 us
    unnamed x16 -> x14, local copies, waits for them, and re-layouts: 1.08 us -> 0.04 us
    ppermute x2, waiting for transfers between devices: 6.55 us -> 5.54 us  [plane_shift(): return lax.ppermute(value, ('row', 'col'), pairs)]
    pallas_call x1, Pallas kernels: 0.31 us -> 1.25 us  [shards(): pl.pallas_call(slab_kernel, out_shape=jax.ShapeDtypeStruct((ROWS * SLAB,...]
    pallas_call x1 -> x2, Pallas kernels: 1.24 us -> 1.99 us  [the longest x1 1 us: shards(): pl.pallas_call(early_kernel, out_shape=jax.ShapeDtypeStruct(band.shape, f...]
  transfers between devices with their start and end apart: 2 -> 2, of which waited for: 2 -> 2; matrix products, arithmetic and copies ran while one was open for 0% -> 0% of each run, Pallas kernels for 2% -> 4%
where the time goes in v3:
time: 51.9 us; the launch traced here: 51.7 us
  blocking collectives  33.5 us (65%)
  starting transfers between devices  7.1 us (14%)
  waiting for transfers between devices  5.54 us (11%)
  Pallas kernels  5.36 us (10%)
    all_to_all x1, blocking collectives, shards(): lax.all_to_all(slabs.reshape(ROWS, 2, 2, 8, LANES), 'col', split_axis=0,...  18.4 us
    all_to_all x1, blocking collectives, shards(): lax.all_to_all(spectra, 'col', split_axis=0, concat_axis=0, tiled=True)  15 us
    ppermute x2, starting transfers between devices, plane_shift(): return lax.ppermute(value, ('row', 'col'), pairs)  7.1 us
    ppermute x2, waiting for transfers between devices, plane_shift(): return lax.ppermute(value, ('row', 'col'), pairs)  5.54 us
    pallas_call x1, Pallas kernels, shards(): pl.pallas_call(slab_kernel, out_shape=jax.ShapeDtypeStruct((ROWS * SLAB,...  1.25 us
    pallas_call x1, Pallas kernels, shards(): pl.pallas_call(transform_kernel, out_shape=jax.ShapeDtypeStruct((ROWS, 2,...  1.12 us
  transfers between devices with their start and end apart: 2, of which 2 were waited for; matrix products, arithmetic and copies ran while one was open for 0% of the time, Pallas kernels for 4%

profile of v3, /device:TPU:96, one launch (start us, length us, event | category | flops | bytes accessed | tf_op | source)
XLA Modules:
  0.0 51.7 jit_solution(14653377366129926731)
XLA Ops:
  0.0 1.3 %slabs.1 = f32[1024,128]{1,0:T(8,128)S(1)} custom-call(f32[2,32,2048]{2,1,0:T(8,128)} %band_ref.1), custom_call_target="tpu_custom_call" | custom-call | tf_op jit(solution)/shard_map/slabs/pallas_call | solution.py:216
  1.3 0.0 copy-start
  1.3 0.0 copy-start.3
  1.3 0.0 copy-start.4
  1.3 18.4 %all_to_all.10.in_ref = f32[32,2,2,8,128]{4,3,2,1,0:T(8,128)S(1)} all-to-all(f32[32,2,2,8,128]{4,3,2,1,0:T(8,128)S(1)} %bitcast.8), channel_id=1, replica_groups=mesh['row'=16,'col'=32] {'col'}, dimensions={0} | all-to-all | bytes 1048576 | tf_op jit(solution)/shard_map/all_to_all | solution.py:227
  19.7 0.0 copy-done
  19.7 0.0 copy-done.3
  19.7 0.0 copy-done.4
  19.7 1.1 %transform.1 = f32[32,2,2,8,128]{4,3,2,1,0:T(8,128)S(1)} custom-call(f32[32,2,2,8,128]{4,3,2,1,0:T(8,128)S(1)} %all_to_all.10.in_ref, bf16[256,512]{1,0:T(8,128)(2,1)S(1)} %copy-done.4, bf16[256,512]{1,0:T(8,128)(2,1)S(1)} %copy-done.3, f32[2,256,256]{2,1,0:T(8,128)S(1)} %copy-done), custom_call_target="tpu_custom_call" | custom-call | tf_op jit(solution)/shard_map/transform/pallas_call | solution.py:230
  20.9 15.0 %all_to_all.11 = f32[32,2,2,8,128]{4,3,2,1,0:T(8,128)S(1)} all-to-all(f32[32,2,2,8,128]{4,3,2,1,0:T(8,128)S(1)} %transform.1), channel_id=1, replica_groups=mesh['row'=16,'col'=32] {'col'}, dimensions={0} | all-to-all | bytes 1048576 | tf_op jit(solution)/shard_map/all_to_all | solution.py:236
  35.9 0.0 copy-start.1
  36.0 5.2 %collective-permute-start = (f32[16,32,128]{2,1,0:T(8,128)S(1)}, f32[16,32,128]{2,1,0:T(8,128)S(1)}, u32[]{:S(2)}, u32[]{:S(2)}) collective-permute-start(f32[16,32,128]{2,1,0:T(8,128)S(1)} %get-tuple-element.13), channel_id=1, source_target_pairs={{0,32},{2,34},{4,36},{6,38},{8,40},{10,42},{12,44},{14,46},{16,48}... | collective-permute-start | bytes 786440 | tf_op jit(solution)/shard_map/ppermute | solution.py:206
  41.2 0.0 copy-start.6
  41.2 0.0 copy-start.5
  41.2 1.9 %collective-permute-start.1 = (f32[16,32,128]{2,1,0:T(8,128)S(1)}, f32[16,32,128]{2,1,0:T(8,128)S(1)}, u32[]{:S(2)}, u32[]{:S(2)}) collective-permute-start(f32[16,32,128]{2,1,0:T(8,128)S(1)} %get-tuple-element.16), channel_id=1, source_target_pairs={{1,33},{3,35},{5,37},{7,39},{9,41},{11,43},{13,45},{15,47},{17,49}... | collective-permute-start | bytes 786440 | tf_op jit(solution)/shard_map/ppermute | solution.py:206
  43.1 0.0 copy-done.1
  43.1 0.0 copy-done.2
  43.1 0.0 copy-done.6
  43.1 0.0 copy-done.5
  43.1 1.0 %turn.1 = (f32[32,2048]{1,0:T(8,128)S(1)}, f32[32,2048]{1,0:T(8,128)S(1)}, s32[32,128]{1,0:T(8,128)S(1)}, f32[128,128]{1,0:T(8,128)S(1)}) custom-call(s32[4,32]{1,0:T(4,128)S(1)} %bitcast.9, f32[4,32]{1,0:T(4,128)S(1)} %bitcast.10, f32[32,2048]{1,0:T(8,128)S(1)} %copy-done.1, f32[32,2048]{1,0:T(8,128)S(1)} %copy-done.2, f32[32,32,128]{2,1,0:T(8,128)S(1)} %bitcast.5), custom_call_target="tpu_custom_call" | custom-call | tf_op jit(solution)/shard_map/turn/pallas_call | solution.py:245
  44.1 2.0 %collective-permute-done.refs_3_ = f32[16,32,128]{2,1,0:T(8,128)S(1)} collective-permute-done((f32[16,32,128]{2,1,0:T(8,128)S(1)}, f32[16,32,128]{2,1,0:T(8,128)S(1)}, u32[]{:S(2)}, u32[]{:S(2)}) %collective-permute-start) | collective-permute-done | bytes 262176 | tf_op jit(solution)/shard_map/ppermute | solution.py:206
  46.1 1.0 %tilt_early.1.early_ref = f32[2,32,2048]{2,1,0:T(8,128)} custom-call(s32[32,128]{1,0:T(8,128)S(1)} %get-tuple-element.11.refs_0_, f32[128,128]{1,0:T(8,128)S(1)} %get-tuple-element.12.refs_1_, f32[32,32,128]{2,1,0:T(8,128)S(1)} %bitcast.6, f32[16,32,128]{2,1,0:T(8,128)S(1)} %collective-permute-done.refs_3_, f32[32,2048]{1,0:T(8,128)S(1)} %get-tuple-element.14.refs_4_, ...), custom_call_target="tpu_custom_call" | custom-call | tf_op jit(solution)/shard_map/tilt_early/pallas_call | solution.py:264
  47.1 3.6 %collective-permute-done.1.refs_3_ = f32[16,32,128]{2,1,0:T(8,128)S(1)} collective-permute-done((f32[16,32,128]{2,1,0:T(8,128)S(1)}, f32[16,32,128]{2,1,0:T(8,128)S(1)}, u32[]{:S(2)}, u32[]{:S(2)}) %collective-permute-start.1) | collective-permute-done | bytes 262176 | tf_op jit(solution)/shard_map/ppermute | solution.py:206
  50.7 1.0 %tilt_late.1 = f32[2,32,2048]{2,1,0:T(8,128)} custom-call(f32[2,32,2048]{2,1,0:T(8,128)} %tilt_early.1.early_ref, s32[32,128]{1,0:T(8,128)S(1)} %get-tuple-element.11.refs_0_, f32[128,128]{1,0:T(8,128)S(1)} %get-tuple-element.12.refs_1_, f32[32,32,128]{2,1,0:T(8,128)S(1)} %bitcast.7, ...), custom_call_target="tpu_custom_call", output_to_operand_aliasing={{}: (0, {})} | custom-call | tf_op jit(solution)/shard_map/tilt_late/pallas_call | solution.py:273
  (2 shorter events, 0.0 us)
Async XLA Ops:
  1.3 18.5 %copy-start = (f32[2,256,256]{2,1,0:T(8,128)S(1)}, f32[2,256,256]{2,1,0:T(8,128)}, u32[]{:S(2)}) copy-start(f32[2,256,256]{2,1,0:T(8,128)} %constant.8.clone.turn_ref) | copy-start | bytes 1572868
  1.3 18.5 %copy-start.3 = (bf16[256,512]{1,0:T(8,128)(2,1)S(1)}, bf16[256,512]{1,0:T(8,128)(2,1)}, u32[]{:S(2)}) copy-start(bf16[256,512]{1,0:T(8,128)(2,1)} %constant.7.clone.lo_ref) | copy-start | bytes 786436
  1.3 18.5 %copy-start.4 = (bf16[256,512]{1,0:T(8,128)(2,1)S(1)}, bf16[256,512]{1,0:T(8,128)(2,1)}, u32[]{:S(2)}) copy-start(bf16[256,512]{1,0:T(8,128)(2,1)} %constant.6.clone.hi_ref) | copy-start | bytes 786436
  35.9 7.2 %copy-start.1 = (f32[32,2048]{1,0:T(8,128)S(1)}, f32[32,2048]{1,0:T(8,128)}, u32[]{:S(2)}) copy-start(f32[32,2048]{1,0:T(8,128)} %jac_ref.1) | copy-start | bytes 786436
  35.9 7.2 %copy-start.2 = (f32[32,2048]{1,0:T(8,128)S(1)}, f32[32,2048]{1,0:T(8,128)}, u32[]{:S(2)}) copy-start(f32[32,2048]{1,0:T(8,128)} %phase_ref.1) | copy-start | bytes 786436
  36.0 10.1 %collective-permute-start = (f32[16,32,128]{2,1,0:T(8,128)S(1)}, f32[16,32,128]{2,1,0:T(8,128)S(1)}, u32[]{:S(2)}, u32[]{:S(2)}) collective-permute-start(f32[16,32,128]{2,1,0:T(8,128)S(1)} %get-tuple-element.13), channel_id=1, source_target_pairs={{0,32},{2,34},{4,36},{6,38},{8,40},{10,42},{12,44},{14,46},{16,48}... | collective-permute-start | bytes 786440 | tf_op jit(solution)/shard_map/ppermute | solution.py:206
  41.2 2.0 %copy-start.6 = (f32[32,4]{0,1:T(4,128)S(1)}, f32[32,4]{0,1:T(4,128)}, u32[]{:S(2)}) copy-start(f32[32,4]{0,1:T(4,128)} %param.10) | copy-start | bytes 1540
  41.2 2.0 %copy-start.5 = (s32[32,4]{0,1:T(4,128)S(1)}, s32[32,4]{0,1:T(4,128)}, u32[]{:S(2)}) copy-start(s32[32,4]{0,1:T(4,128)} %param.9) | copy-start | bytes 1540
  41.2 9.5 %collective-permute-start.1 = (f32[16,32,128]{2,1,0:T(8,128)S(1)}, f32[16,32,128]{2,1,0:T(8,128)S(1)}, u32[]{:S(2)}, u32[]{:S(2)}) collective-permute-start(f32[16,32,128]{2,1,0:T(8,128)S(1)} %get-tuple-element.16), channel_id=1, source_target_pairs={{1,33},{3,35},{5,37},{7,39},{9,41},{11,43},{13,45},{15,47},{17,49}... | collective-permute-start | bytes 786440 | tf_op jit(solution)/shard_map/ppermute | solution.py:206

commit v4 on v3

--- a/solution.py
+++ b/solution.py
@@ -117,8 +117,12 @@
             out_ref[:, c, h] = final[:, start : start + LANES].reshape(ROWS, 8, LANES)
 
 
-def core_parity():
-    return lax.axis_index("col") % 2
+def above_first(plane, core):
+    return (plane + core + 1) % 2
+
+
+def my_above_first():
+    return above_first(lax.axis_index("row"), lax.axis_index("col"))
 
 
 def border_kernel(own_ref, first_ref, second_ref):
@@ -126,9 +130,9 @@
         last_ref[...] = own_ref[ROWS - HALO :]
         initial_ref[...] = own_ref[:HALO]
 
-    parity = core_parity()
-    pl.when(parity == 0)(lambda: put(first_ref, second_ref))
-    pl.when(parity == 1)(lambda: put(second_ref, first_ref))
+    above = my_above_first()
+    pl.when(above == 1)(lambda: put(first_ref, second_ref))
+    pl.when(above == 0)(lambda: put(second_ref, first_ref))
 
 
 def turn_kernel(sources_ref, taps_ref, jac_ref, phase_ref, own_ref, cos_ref, sin_ref, base_ref, weight_ref):
@@ -148,7 +152,7 @@
 
 
 def tilt_half(late, base_ref, weight_ref, own_ref, halo_ref, cos_ref, sin_ref, out_ref, ext, total, held, sems):
-    half = (core_parity() + late) % 2
+    half = (my_above_first() + late) % 2
 
     @pl.when(half == 0)
     def _():
@@ -195,12 +199,12 @@
     tilt_half(1, *refs)
 
 
-def plane_shift(value, even_step):
+def swap(value, late):
     planes, columns = lax.axis_size("row"), lax.axis_size("col")
     pairs = []
     for g in range(planes):
         for c in range(columns):
-            to = g + (even_step if c % 2 == 0 else -even_step)
+            to = g + (1 if above_first(g, c) != late else -1)
             if 0 <= to < planes:
                 pairs.append((g * columns + c, to * columns + c))
     return lax.ppermute(value, ("row", "col"), pairs)
@@ -239,8 +243,8 @@
     first, second = pl.pallas_call(
         border_kernel, out_shape=[border, border], name="border_rows", compiler_params=limit
     )(own)
-    first = plane_shift(first, 1)
-    second = plane_shift(second, -1)
+    first = swap(first, 0)
+    second = swap(second, 1)
     weights = jax.ShapeDtypeStruct(jacobian.shape, f32)
     cosine, sine, base, weight = pl.pallas_call(
         turn_kernel,

time: 51.9 us -> 50.7 us (0.977)
  the two profiles are of different devices: /device:TPU:96 before, /device:TPU:128 now
where the time goes in v4:
time: 50.7 us; the launch traced here: 50.4 us
  blocking collectives  33.5 us (66%)
  starting transfers between devices  5.86 us (12%)
  waiting for transfers between devices  5.54 us (11%)
  Pallas kernels  5.35 us (11%)
    all_to_all x1, blocking collectives, shards(): lax.all_to_all(slabs.reshape(ROWS, 2, 2, 8, LANES), 'col', split_axis=0,...  18.4 us
    all_to_all x1, blocking collectives, shards(): lax.all_to_all(spectra, 'col', split_axis=0, concat_axis=0, tiled=True)  15.1 us
    ppermute x2, starting transfers between devices, swap(): return lax.ppermute(value, ('row', 'col'), pairs)  5.86 us
    ppermute x2, waiting for transfers between devices, swap(): return lax.ppermute(value, ('row', 'col'), pairs)  5.54 us
    pallas_call x1, Pallas kernels, shards(): pl.pallas_call(slab_kernel, out_shape=jax.ShapeDtypeStruct((ROWS * SLAB,...  1.25 us
    pallas_call x1, Pallas kernels, shards(): pl.pallas_call(transform_kernel, out_shape=jax.ShapeDtypeStruct((ROWS, 2,...  1.12 us
  transfers between devices with their start and end apart: 2, of which 2 were waited for; matrix products, arithmetic and copies ran while one was open for 0% of the time, Pallas kernels for 4%

profile of v4, /device:TPU:128, one launch (start us, length us, event | category | flops | bytes accessed | tf_op | source)
XLA Modules:
  0.0 50.4 jit_solution(9603945166662014148)
XLA Ops:
  0.0 1.3 %slabs.1 = f32[1024,128]{1,0:T(8,128)S(1)} custom-call(f32[2,32,2048]{2,1,0:T(8,128)} %band_ref.1), custom_call_target="tpu_custom_call" | custom-call | tf_op jit(solution)/shard_map/slabs/pallas_call | solution.py:220
  1.3 0.0 copy-start
  1.3 0.0 copy-start.3
  1.3 0.0 copy-start.4
  1.3 18.4 %all_to_all.10.in_ref = f32[32,2,2,8,128]{4,3,2,1,0:T(8,128)S(1)} all-to-all(f32[32,2,2,8,128]{4,3,2,1,0:T(8,128)S(1)} %bitcast.8), channel_id=1, replica_groups=mesh['row'=16,'col'=32] {'col'}, dimensions={0} | all-to-all | bytes 1048576 | tf_op jit(solution)/shard_map/all_to_all | solution.py:231
  19.7 0.0 copy-done
  19.7 0.0 copy-done.3
  19.7 0.0 copy-done.4
  19.7 1.1 %transform.1 = f32[32,2,2,8,128]{4,3,2,1,0:T(8,128)S(1)} custom-call(f32[32,2,2,8,128]{4,3,2,1,0:T(8,128)S(1)} %all_to_all.10.in_ref, bf16[256,512]{1,0:T(8,128)(2,1)S(1)} %copy-done.4, bf16[256,512]{1,0:T(8,128)(2,1)S(1)} %copy-done.3, f32[2,256,256]{2,1,0:T(8,128)S(1)} %copy-done), custom_call_target="tpu_custom_call" | custom-call | tf_op jit(solution)/shard_map/transform/pallas_call | solution.py:234
  20.9 15.1 %all_to_all.11 = f32[32,2,2,8,128]{4,3,2,1,0:T(8,128)S(1)} all-to-all(f32[32,2,2,8,128]{4,3,2,1,0:T(8,128)S(1)} %transform.1), channel_id=1, replica_groups=mesh['row'=16,'col'=32] {'col'}, dimensions={0} | all-to-all | bytes 1048576 | tf_op jit(solution)/shard_map/all_to_all | solution.py:240
  35.9 0.0 copy-start.1
  36.0 3.9 %collective-permute-start = (f32[16,32,128]{2,1,0:T(8,128)S(1)}, f32[16,32,128]{2,1,0:T(8,128)S(1)}, u32[]{:S(2)}, u32[]{:S(2)}) collective-permute-start(f32[16,32,128]{2,1,0:T(8,128)S(1)} %get-tuple-element.13), channel_id=1, source_target_pairs={{0,32},{2,34},{4,36},{6,38},{8,40},{10,42},{12,44},{14,46},{16,48}... | collective-permute-start | bytes 786440 | tf_op jit(solution)/shard_map/ppermute | solution.py:210
  39.9 0.0 copy-start.6
  39.9 0.0 copy-start.5
  40.0 1.9 %collective-permute-start.1 = (f32[16,32,128]{2,1,0:T(8,128)S(1)}, f32[16,32,128]{2,1,0:T(8,128)S(1)}, u32[]{:S(2)}, u32[]{:S(2)}) collective-permute-start(f32[16,32,128]{2,1,0:T(8,128)S(1)} %get-tuple-element.16), channel_id=1, source_target_pairs={{1,33},{3,35},{5,37},{7,39},{9,41},{11,43},{13,45},{15,47},{17,49}... | collective-permute-start | bytes 786440 | tf_op jit(solution)/shard_map/ppermute | solution.py:210
  41.9 0.0 copy-done.1
  41.9 0.0 copy-done.2
  41.9 0.0 copy-done.6
  41.9 0.0 copy-done.5
  41.9 1.0 %turn.1 = (f32[32,2048]{1,0:T(8,128)S(1)}, f32[32,2048]{1,0:T(8,128)S(1)}, s32[32,128]{1,0:T(8,128)S(1)}, f32[128,128]{1,0:T(8,128)S(1)}) custom-call(s32[4,32]{1,0:T(4,128)S(1)} %bitcast.9, f32[4,32]{1,0:T(4,128)S(1)} %bitcast.10, f32[32,2048]{1,0:T(8,128)S(1)} %copy-done.1, f32[32,2048]{1,0:T(8,128)S(1)} %copy-done.2, f32[32,32,128]{2,1,0:T(8,128)S(1)} %bitcast.5), custom_call_target="tpu_custom_call" | custom-call | tf_op jit(solution)/shard_map/turn/pallas_call | solution.py:249
  42.9 1.5 %collective-permute-done.refs_3_ = f32[16,32,128]{2,1,0:T(8,128)S(1)} collective-permute-done((f32[16,32,128]{2,1,0:T(8,128)S(1)}, f32[16,32,128]{2,1,0:T(8,128)S(1)}, u32[]{:S(2)}, u32[]{:S(2)}) %collective-permute-start) | collective-permute-done | bytes 262176 | tf_op jit(solution)/shard_map/ppermute | solution.py:210
  44.4 1.0 %tilt_early.1.early_ref = f32[2,32,2048]{2,1,0:T(8,128)} custom-call(s32[32,128]{1,0:T(8,128)S(1)} %get-tuple-element.11.refs_0_, f32[128,128]{1,0:T(8,128)S(1)} %get-tuple-element.12.refs_1_, f32[32,32,128]{2,1,0:T(8,128)S(1)} %bitcast.6, f32[16,32,128]{2,1,0:T(8,128)S(1)} %collective-permute-done.refs_3_, f32[32,2048]{1,0:T(8,128)S(1)} %get-tuple-element.14.refs_4_, ...), custom_call_target="tpu_custom_call" | custom-call | tf_op jit(solution)/shard_map/tilt_early/pallas_call | solution.py:268
  45.4 4.1 %collective-permute-done.1.refs_3_ = f32[16,32,128]{2,1,0:T(8,128)S(1)} collective-permute-done((f32[16,32,128]{2,1,0:T(8,128)S(1)}, f32[16,32,128]{2,1,0:T(8,128)S(1)}, u32[]{:S(2)}, u32[]{:S(2)}) %collective-permute-start.1) | collective-permute-done | bytes 262176 | tf_op jit(solution)/shard_map/ppermute | solution.py:210
  49.4 1.0 %tilt_late.1 = f32[2,32,2048]{2,1,0:T(8,128)} custom-call(f32[2,32,2048]{2,1,0:T(8,128)} %tilt_early.1.early_ref, s32[32,128]{1,0:T(8,128)S(1)} %get-tuple-element.11.refs_0_, f32[128,128]{1,0:T(8,128)S(1)} %get-tuple-element.12.refs_1_, f32[32,32,128]{2,1,0:T(8,128)S(1)} %bitcast.7, ...), custom_call_target="tpu_custom_call", output_to_operand_aliasing={{}: (0, {})} | custom-call | tf_op jit(solution)/shard_map/tilt_late/pallas_call | solution.py:277
  (2 shorter events, 0.0 us)
Async XLA Ops:
  1.3 18.5 %copy-start = (f32[2,256,256]{2,1,0:T(8,128)S(1)}, f32[2,256,256]{2,1,0:T(8,128)}, u32[]{:S(2)}) copy-start(f32[2,256,256]{2,1,0:T(8,128)} %constant.8.clone.turn_ref) | copy-start | bytes 1572868
  1.3 18.5 %copy-start.3 = (bf16[256,512]{1,0:T(8,128)(2,1)S(1)}, bf16[256,512]{1,0:T(8,128)(2,1)}, u32[]{:S(2)}) copy-start(bf16[256,512]{1,0:T(8,128)(2,1)} %constant.7.clone.lo_ref) | copy-start | bytes 786436
  1.3 18.5 %copy-start.4 = (bf16[256,512]{1,0:T(8,128)(2,1)S(1)}, bf16[256,512]{1,0:T(8,128)(2,1)}, u32[]{:S(2)}) copy-start(bf16[256,512]{1,0:T(8,128)(2,1)} %constant.6.clone.hi_ref) | copy-start | bytes 786436
  35.9 6.0 %copy-start.1 = (f32[32,2048]{1,0:T(8,128)S(1)}, f32[32,2048]{1,0:T(8,128)}, u32[]{:S(2)}) copy-start(f32[32,2048]{1,0:T(8,128)} %jac_ref.1) | copy-start | bytes 786436
  35.9 6.0 %copy-start.2 = (f32[32,2048]{1,0:T(8,128)S(1)}, f32[32,2048]{1,0:T(8,128)}, u32[]{:S(2)}) copy-start(f32[32,2048]{1,0:T(8,128)} %phase_ref.1) | copy-start | bytes 786436
  36.0 8.4 %collective-permute-start = (f32[16,32,128]{2,1,0:T(8,128)S(1)}, f32[16,32,128]{2,1,0:T(8,128)S(1)}, u32[]{:S(2)}, u32[]{:S(2)}) collective-permute-start(f32[16,32,128]{2,1,0:T(8,128)S(1)} %get-tuple-element.13), channel_id=1, source_target_pairs={{0,32},{2,34},{4,36},{6,38},{8,40},{10,42},{12,44},{14,46},{16,48}... | collective-permute-start | bytes 786440 | tf_op jit(solution)/shard_map/ppermute | solution.py:210
  39.9 2.0 %copy-start.6 = (f32[32,4]{0,1:T(4,128)S(1)}, f32[32,4]{0,1:T(4,128)}, u32[]{:S(2)}) copy-start(f32[32,4]{0,1:T(4,128)} %param.10) | copy-start | bytes 1540
  39.9 2.0 %copy-start.5 = (s32[32,4]{0,1:T(4,128)S(1)}, s32[32,4]{0,1:T(4,128)}, u32[]{:S(2)}) copy-start(s32[32,4]{0,1:T(4,128)} %param.9) | copy-start | bytes 1540
  40.0 9.5 %collective-permute-start.1 = (f32[16,32,128]{2,1,0:T(8,128)S(1)}, f32[16,32,128]{2,1,0:T(8,128)S(1)}, u32[]{:S(2)}, u32[]{:S(2)}) collective-permute-start(f32[16,32,128]{2,1,0:T(8,128)S(1)} %get-tuple-element.16), channel_id=1, source_target_pairs={{1,33},{3,35},{5,37},{7,39},{9,41},{11,43},{13,45},{15,47},{17,49}... | collective-permute-start | bytes 786440 | tf_op jit(solution)/shard_map/ppermute | solution.py:210

commit v5 on v4

--- a/solution.py
+++ b/solution.py
@@ -151,8 +151,29 @@
             )
 
 
-def tilt_half(late, base_ref, weight_ref, own_ref, halo_ref, cos_ref, sin_ref, out_ref, ext, total, held, sems):
-    half = (my_above_first() + late) % 2
+def turn_out(group, offset, total, cos_ref, sin_ref, held, out_ref, sems):
+    rows = pl.ds(pl.multiple_of(offset + 8 * group, 8), 8)
+    for tile in range(TILES):
+        columns = slice(tile * LANES, (tile + 1) * LANES)
+        start = 8 * group * SLAB + tile_start(tile)
+        re = total[pl.ds(start, 8, stride=SLAB), :]
+        im = total[pl.ds(16 + start, 8, stride=SLAB), :]
+        cosine, sine = cos_ref[rows, columns], sin_ref[rows, columns]
+        held[group, 0, :, columns] = re * cosine - im * sine
+        held[group, 1, :, columns] = re * sine + im * cosine
+    copy = pltpu.make_async_copy(held.at[group], out_ref.at[:, rows], sems.at[group])
+    copy.start()
+    return copy
+
+
+def row_terms(base_ref, weight_ref, offset, r):
+    base = base_ref[pl.ds(offset + r, 1), :]
+    weights = weight_ref[pl.ds(pl.multiple_of(4 * offset, 4 * HALO) + 4 * r, 4), :]
+    return base, base[0:1, 0:1][0, 0], weights
+
+
+def early_kernel(base_ref, weight_ref, own_ref, halo_ref, cos_ref, sin_ref, out_ref, part_ref, ext, total, held, sems):
+    half = my_above_first()
 
     @pl.when(half == 0)
     def _():
@@ -168,35 +189,46 @@
     copies = []
     for group in range(HALF_GROUPS):
         for r in range(8 * group, 8 * group + 8):
-            base = base_ref[pl.ds(offset + r, 1), 0:1][0, 0]
-            weights = weight_ref[pl.ds(pl.multiple_of(4 * offset, 4 * HALO) + 4 * r, 4), :]
+            _, base, weights = row_terms(base_ref, weight_ref, offset, r)
             acc = weights[0:1] * ext[base]
             for j in range(1, 4):
                 acc = acc + weights[j : j + 1] * ext[base + j]
             total[r * SLAB : (r + 1) * SLAB, :] = acc
-        rows = pl.ds(pl.multiple_of(offset + 8 * group, 8), 8)
-        for tile in range(TILES):
-            columns = slice(tile * LANES, (tile + 1) * LANES)
-            start = 8 * group * SLAB + tile_start(tile)
-            re = total[pl.ds(start, 8, stride=SLAB), :]
-            im = total[pl.ds(16 + start, 8, stride=SLAB), :]
-            cosine, sine = cos_ref[rows, columns], sin_ref[rows, columns]
-            held[group, 0, :, columns] = re * cosine - im * sine
-            held[group, 1, :, columns] = re * sine + im * cosine
-        copies.append(
-            pltpu.make_async_copy(held.at[group], out_ref.at[:, rows], sems.at[group])
-        )
-        copies[-1].start()
+        copies.append(turn_out(group, offset, total, cos_ref, sin_ref, held, out_ref, sems))
+    other = 1 - half
+    first_own = HALO * (1 - other)
+    offset = pl.multiple_of(other * HALO, HALO)
+    for r in range(HALO):
+        rows, base, weights = row_terms(base_ref, weight_ref, offset, r)
+        acc = jnp.zeros((SLAB, LANES), jnp.float32)
+        for j in range(4):
+            place = rows + (j - first_own)
+            inside = jnp.logical_and(place >= 0, place < ROWS)
+            tap = jnp.where(inside, weights[j : j + 1], 0.0)
+            acc = acc + tap * own_ref[jnp.clip(base + j - first_own, 0, ROWS - 1)]
+        part_ref[r * SLAB : (r + 1) * SLAB, :] = acc
     for copy in copies:
         copy.wait()
 
 
-def early_kernel(*refs):
-    tilt_half(0, *refs)
-
-
-def late_kernel(early_ref, *refs):
-    tilt_half(1, *refs)
+def late_kernel(early_ref, base_ref, weight_ref, part_ref, halo_ref, cos_ref, sin_ref, out_ref, total, held, sems):
+    half = 1 - my_above_first()
+    first_halo = ROWS * half
+    offset = pl.multiple_of(half * HALO, HALO)
+    copies = []
+    for group in range(HALF_GROUPS):
+        for r in range(8 * group, 8 * group + 8):
+            rows, base, weights = row_terms(base_ref, weight_ref, offset, r)
+            acc = part_ref[r * SLAB : (r + 1) * SLAB, :]
+            for j in range(4):
+                place = rows + (j - first_halo)
+                inside = jnp.logical_and(place >= 0, place < HALO)
+                tap = jnp.where(inside, weights[j : j + 1], 0.0)
+                acc = acc + tap * halo_ref[jnp.clip(base + j - first_halo, 0, HALO - 1)]
+            total[r * SLAB : (r + 1) * SLAB, :] = acc
+        copies.append(turn_out(group, offset, total, cos_ref, sin_ref, held, out_ref, sems))
+    for copy in copies:
+        copy.wait()
 
 
 def swap(value, late):
@@ -260,17 +292,19 @@
     )(sources.T, taps.T, jacobian, phase, own)
     any_space = pl.BlockSpec(memory_space=pl.ANY)
     scratch = [
-        pltpu.VMEM((ROWS + HALO, SLAB, LANES), f32),
         pltpu.VMEM((HALO * SLAB, LANES), f32),
         pltpu.VMEM((HALF_GROUPS, 2, 8, TILES * LANES), f32),
         pltpu.SemaphoreType.DMA((HALF_GROUPS,)),
     ]
-    early = pl.pallas_call(
+    early, part = pl.pallas_call(
         early_kernel,
-        out_shape=jax.ShapeDtypeStruct(band.shape, f32),
+        out_shape=[
+            jax.ShapeDtypeStruct(band.shape, f32),
+            jax.ShapeDtypeStruct((HALO * SLAB, LANES), f32),
+        ],
         in_specs=[vmem] * 6,
-        out_specs=hbm,
-        scratch_shapes=scratch,
+        out_specs=[hbm, vmem],
+        scratch_shapes=[pltpu.VMEM((ROWS + HALO, SLAB, LANES), f32)] + scratch,
         name="tilt_early",
         compiler_params=limit,
     )(base, weight, own, first, cosine, sine)
@@ -283,7 +317,7 @@
         scratch_shapes=scratch,
         name="tilt_late",
         compiler_params=limit,
-    )(early, base, weight, own, second, cosine, sine)
+    )(early, base, weight, part, second, cosine, sine)
 
 
 def solution(mesh):

time: 50.7 us -> 50.7 us (level)
  no operation moved by 1% of the time
where the time goes in v5:
time: 50.7 us; the launch traced here: 50.5 us
  blocking collectives  33.5 us (66%)
  starting transfers between devices  5.86 us (12%)
  Pallas kernels  5.56 us (11%)
  waiting for transfers between devices  5.37 us (11%)
    all_to_all x1, blocking collectives, shards(): lax.all_to_all(slabs.reshape(ROWS, 2, 2, 8, LANES), 'col', split_axis=0,...  18.4 us
    all_to_all x1, blocking collectives, shards(): lax.all_to_all(spectra, 'col', split_axis=0, concat_axis=0, tiled=True)  15.1 us
    ppermute x2, starting transfers between devices, swap(): return lax.ppermute(value, ('row', 'col'), pairs)  5.86 us
    ppermute x2, waiting for transfers between devices, swap(): return lax.ppermute(value, ('row', 'col'), pairs)  5.37 us
    pallas_call x1, Pallas kernels, shards(): pl.pallas_call(slab_kernel, out_shape=jax.ShapeDtypeStruct((ROWS * SLAB,...  1.25 us
    pallas_call x1, Pallas kernels, shards(): pl.pallas_call(early_kernel, out_shape=[jax.ShapeDtypeStruct(band.shape,...  1.17 us
    pallas_call x1, Pallas kernels, shards(): pl.pallas_call(transform_kernel, out_shape=jax.ShapeDtypeStruct((ROWS, 2,...  1.12 us
    pallas_call x1, Pallas kernels, shards(): pl.pallas_call(late_kernel, out_shape=jax.ShapeDtypeStruct(band.shape, f3...  1.03 us
  transfers between devices with their start and end apart: 2, of which 2 were waited for; matrix products, arithmetic and copies ran while one was open for 0% of the time, Pallas kernels for 4%

profile of v5, /device:TPU:128, one launch (start us, length us, event | category | flops | bytes accessed | tf_op | source)
XLA Modules:
  0.0 50.5 jit_solution(5846324337428617302)
XLA Ops:
  0.0 1.3 %slabs.1 = f32[1024,128]{1,0:T(8,128)S(1)} custom-call(f32[2,32,2048]{2,1,0:T(8,128)} %band_ref.1), custom_call_target="tpu_custom_call" | custom-call | tf_op jit(solution)/shard_map/slabs/pallas_call | solution.py:252
  1.3 0.0 copy-start
  1.3 0.0 copy-start.3
  1.3 0.0 copy-start.4
  1.3 18.4 %all_to_all.10.in_ref = f32[32,2,2,8,128]{4,3,2,1,0:T(8,128)S(1)} all-to-all(f32[32,2,2,8,128]{4,3,2,1,0:T(8,128)S(1)} %bitcast.7), channel_id=1, replica_groups=mesh['row'=16,'col'=32] {'col'}, dimensions={0} | all-to-all | bytes 1048576 | tf_op jit(solution)/shard_map/all_to_all | solution.py:263
  19.7 0.0 copy-done
  19.7 0.0 copy-done.3
  19.7 0.0 copy-done.4
  19.7 1.1 %transform.1 = f32[32,2,2,8,128]{4,3,2,1,0:T(8,128)S(1)} custom-call(f32[32,2,2,8,128]{4,3,2,1,0:T(8,128)S(1)} %all_to_all.10.in_ref, bf16[256,512]{1,0:T(8,128)(2,1)S(1)} %copy-done.4, bf16[256,512]{1,0:T(8,128)(2,1)S(1)} %copy-done.3, f32[2,256,256]{2,1,0:T(8,128)S(1)} %copy-done), custom_call_target="tpu_custom_call" | custom-call | tf_op jit(solution)/shard_map/transform/pallas_call | solution.py:266
  20.9 15.1 %all_to_all.11 = f32[32,2,2,8,128]{4,3,2,1,0:T(8,128)S(1)} all-to-all(f32[32,2,2,8,128]{4,3,2,1,0:T(8,128)S(1)} %transform.1), channel_id=1, replica_groups=mesh['row'=16,'col'=32] {'col'}, dimensions={0} | all-to-all | bytes 1048576 | tf_op jit(solution)/shard_map/all_to_all | solution.py:272
  35.9 0.0 copy-start.2
  36.0 3.9 %collective-permute-start = (f32[16,32,128]{2,1,0:T(8,128)S(1)}, f32[16,32,128]{2,1,0:T(8,128)S(1)}, u32[]{:S(2)}, u32[]{:S(2)}) collective-permute-start(f32[16,32,128]{2,1,0:T(8,128)S(1)} %get-tuple-element.15), channel_id=1, source_target_pairs={{0,32},{2,34},{4,36},{6,38},{8,40},{10,42},{12,44},{14,46},{16,48}... | collective-permute-start | bytes 786440 | tf_op jit(solution)/shard_map/ppermute | solution.py:242
  39.9 0.0 copy-start.6
  39.9 0.0 copy-start.5
  40.0 1.9 %collective-permute-start.1 = (f32[16,32,128]{2,1,0:T(8,128)S(1)}, f32[16,32,128]{2,1,0:T(8,128)S(1)}, u32[]{:S(2)}, u32[]{:S(2)}) collective-permute-start(f32[16,32,128]{2,1,0:T(8,128)S(1)} %get-tuple-element.20), channel_id=1, source_target_pairs={{1,33},{3,35},{5,37},{7,39},{9,41},{11,43},{13,45},{15,47},{17,49}... | collective-permute-start | bytes 786440 | tf_op jit(solution)/shard_map/ppermute | solution.py:242
  41.9 0.0 copy-done.1
  41.9 0.0 copy-done.2
  41.9 0.0 copy-done.6
  41.9 0.0 copy-done.5
  41.9 1.0 %turn.1 = (f32[32,2048]{1,0:T(8,128)S(1)}, f32[32,2048]{1,0:T(8,128)S(1)}, s32[32,128]{1,0:T(8,128)S(1)}, f32[128,128]{1,0:T(8,128)S(1)}) custom-call(s32[4,32]{1,0:T(4,128)S(1)} %bitcast.8, f32[4,32]{1,0:T(4,128)S(1)} %bitcast.9, f32[32,2048]{1,0:T(8,128)S(1)} %copy-done.1, f32[32,2048]{1,0:T(8,128)S(1)} %copy-done.2, f32[32,32,128]{2,1,0:T(8,128)S(1)} %bitcast.5), custom_call_target="tpu_custom_call" | custom-call | tf_op jit(solution)/shard_map/turn/pallas_call | solution.py:281
  42.9 1.5 %collective-permute-done.halo_ref = f32[16,32,128]{2,1,0:T(8,128)S(1)} collective-permute-done((f32[16,32,128]{2,1,0:T(8,128)S(1)}, f32[16,32,128]{2,1,0:T(8,128)S(1)}, u32[]{:S(2)}, u32[]{:S(2)}) %collective-permute-start) | collective-permute-done | bytes 262176 | tf_op jit(solution)/shard_map/ppermute | solution.py:242
  44.4 1.2 %tilt_early.1 = (f32[2,32,2048]{2,1,0:T(8,128)}, f32[512,128]{1,0:T(8,128)S(1)}) custom-call(s32[32,128]{1,0:T(8,128)S(1)} %get-tuple-element.13.base_ref, f32[128,128]{1,0:T(8,128)S(1)} %get-tuple-element.14.weight_ref, f32[32,32,128]{2,1,0:T(8,128)S(1)} %bitcast.6, f32[16,32,128]{2,1,0:T(8,128)S(1)} %collective-permute-done.halo_ref, ...), custom_call_target="tpu_custom_call" | custom-call | tf_op jit(solution)/shard_map/tilt_early/pallas_call | solution.py:299
  45.6 3.9 %collective-permute-done.1.halo_ref = f32[16,32,128]{2,1,0:T(8,128)S(1)} collective-permute-done((f32[16,32,128]{2,1,0:T(8,128)S(1)}, f32[16,32,128]{2,1,0:T(8,128)S(1)}, u32[]{:S(2)}, u32[]{:S(2)}) %collective-permute-start.1) | collective-permute-done | bytes 262176 | tf_op jit(solution)/shard_map/ppermute | solution.py:242
  49.4 1.0 %tilt_late.1 = f32[2,32,2048]{2,1,0:T(8,128)} custom-call(f32[2,32,2048]{2,1,0:T(8,128)} %get-tuple-element.18.early_ref, s32[32,128]{1,0:T(8,128)S(1)} %get-tuple-element.13.base_ref, f32[128,128]{1,0:T(8,128)S(1)} %get-tuple-element.14.weight_ref, f32[512,128]{1,0:T(8,128)S(1)} %get-tuple-element.19.part_ref, ...), custom_call_target="tpu_custom_call", output_to_operand_aliasing={{}: (0, {})} | custom-call | tf_op jit(solution)/shard_map/tilt_late/pallas_call | solution.py:311
  (2 shorter events, 0.0 us)
Async XLA Ops:
  1.3 18.5 %copy-start = (f32[2,256,256]{2,1,0:T(8,128)S(1)}, f32[2,256,256]{2,1,0:T(8,128)}, u32[]{:S(2)}) copy-start(f32[2,256,256]{2,1,0:T(8,128)} %constant.8.clone.turn_ref) | copy-start | bytes 1572868
  1.3 18.5 %copy-start.3 = (bf16[256,512]{1,0:T(8,128)(2,1)S(1)}, bf16[256,512]{1,0:T(8,128)(2,1)}, u32[]{:S(2)}) copy-start(bf16[256,512]{1,0:T(8,128)(2,1)} %constant.7.clone.lo_ref) | copy-start | bytes 786436
  1.3 18.5 %copy-start.4 = (bf16[256,512]{1,0:T(8,128)(2,1)S(1)}, bf16[256,512]{1,0:T(8,128)(2,1)}, u32[]{:S(2)}) copy-start(bf16[256,512]{1,0:T(8,128)(2,1)} %constant.6.clone.hi_ref) | copy-start | bytes 786436
  35.9 6.0 %copy-start.1 = (f32[32,2048]{1,0:T(8,128)S(1)}, f32[32,2048]{1,0:T(8,128)}, u32[]{:S(2)}) copy-start(f32[32,2048]{1,0:T(8,128)} %jac_ref.1) | copy-start | bytes 786436
  35.9 6.0 %copy-start.2 = (f32[32,2048]{1,0:T(8,128)S(1)}, f32[32,2048]{1,0:T(8,128)}, u32[]{:S(2)}) copy-start(f32[32,2048]{1,0:T(8,128)} %phase_ref.1) | copy-start | bytes 786436
  36.0 8.4 %collective-permute-start = (f32[16,32,128]{2,1,0:T(8,128)S(1)}, f32[16,32,128]{2,1,0:T(8,128)S(1)}, u32[]{:S(2)}, u32[]{:S(2)}) collective-permute-start(f32[16,32,128]{2,1,0:T(8,128)S(1)} %get-tuple-element.15), channel_id=1, source_target_pairs={{0,32},{2,34},{4,36},{6,38},{8,40},{10,42},{12,44},{14,46},{16,48}... | collective-permute-start | bytes 786440 | tf_op jit(solution)/shard_map/ppermute | solution.py:242
  39.9 2.0 %copy-start.6 = (f32[32,4]{0,1:T(4,128)S(1)}, f32[32,4]{0,1:T(4,128)}, u32[]{:S(2)}) copy-start(f32[32,4]{0,1:T(4,128)} %param.10) | copy-start | bytes 1540
  39.9 2.0 %copy-start.5 = (s32[32,4]{0,1:T(4,128)S(1)}, s32[32,4]{0,1:T(4,128)}, u32[]{:S(2)}) copy-start(s32[32,4]{0,1:T(4,128)} %param.9) | copy-start | bytes 1540
  40.0 9.5 %collective-permute-start.1 = (f32[16,32,128]{2,1,0:T(8,128)S(1)}, f32[16,32,128]{2,1,0:T(8,128)S(1)}, u32[]{:S(2)}, u32[]{:S(2)}) collective-permute-start(f32[16,32,128]{2,1,0:T(8,128)S(1)} %get-tuple-element.20), channel_id=1, source_target_pairs={{1,33},{3,35},{5,37},{7,39},{9,41},{11,43},{13,45},{15,47},{17,49}... | collective-permute-start | bytes 786440 | tf_op jit(solution)/shard_map/ppermute | solution.py:242

commit v6 on v4

--- a/solution.py
+++ b/solution.py
@@ -12,6 +12,7 @@
 LANES = 128
 ROWS = 32
 HALO = 16
+PIECE = 8
 TILES = 16
 HALF_GROUPS = 2
 GROUPS = 4
@@ -183,10 +184,16 @@
             cosine, sine = cos_ref[rows, columns], sin_ref[rows, columns]
             held[group, 0, :, columns] = re * cosine - im * sine
             held[group, 1, :, columns] = re * sine + im * cosine
-        copies.append(
-            pltpu.make_async_copy(held.at[group], out_ref.at[:, rows], sems.at[group])
-        )
-        copies[-1].start()
+            if tile % PIECE == PIECE - 1:
+                piece = slice((tile + 1 - PIECE) * LANES, (tile + 1) * LANES)
+                copies.append(
+                    pltpu.make_async_copy(
+                        held.at[group, :, :, piece],
+                        out_ref.at[:, rows, piece],
+                        sems.at[len(copies)],
+                    )
+                )
+                copies[-1].start()
     for copy in copies:
         copy.wait()
 
@@ -263,7 +270,7 @@
         pltpu.VMEM((ROWS + HALO, SLAB, LANES), f32),
         pltpu.VMEM((HALO * SLAB, LANES), f32),
         pltpu.VMEM((HALF_GROUPS, 2, 8, TILES * LANES), f32),
-        pltpu.SemaphoreType.DMA((HALF_GROUPS,)),
+        pltpu.SemaphoreType.DMA((HALF_GROUPS * TILES // PIECE,)),
     ]
     early = pl.pallas_call(
         early_kernel,

time: 50.7 us -> 50.7 us (level)
  no operation moved by 1% of the time
where the time goes in v6:
time: 50.7 us; the launch traced here: 50.4 us
  blocking collectives  33.5 us (66%)
  starting transfers between devices  5.86 us (12%)
  waiting for transfers between devices  5.53 us (11%)
  Pallas kernels  5.37 us (11%)
    all_to_all x1, blocking collectives, shards(): lax.all_to_all(slabs.reshape(ROWS, 2, 2, 8, LANES), 'col', split_axis=0,...  18.4 us
    all_to_all x1, blocking collectives, shards(): lax.all_to_all(spectra, 'col', split_axis=0, concat_axis=0, tiled=True)  15.1 us
    ppermute x2, starting transfers between devices, swap(): return lax.ppermute(value, ('row', 'col'), pairs)  5.86 us
    ppermute x2, waiting for transfers between devices, swap(): return lax.ppermute(value, ('row', 'col'), pairs)  5.53 us
    pallas_call x1, Pallas kernels, shards(): pl.pallas_call(slab_kernel, out_shape=jax.ShapeDtypeStruct((ROWS * SLAB,...  1.25 us
    pallas_call x1, Pallas kernels, shards(): pl.pallas_call(transform_kernel, out_shape=jax.ShapeDtypeStruct((ROWS, 2,...  1.12 us
  transfers between devices with their start and end apart: 2, of which 2 were waited for; matrix products, arithmetic and copies ran while one was open for 0% of the time, Pallas kernels for 4%

profile of v6, /device:TPU:128, one launch (start us, length us, event | category | flops | bytes accessed | tf_op | source)
XLA Modules:
  0.0 50.4 jit_solution(1793350995119572653)
XLA Ops:
  0.0 1.3 %slabs.1 = f32[1024,128]{1,0:T(8,128)S(1)} custom-call(f32[2,32,2048]{2,1,0:T(8,128)} %band_ref.1), custom_call_target="tpu_custom_call" | custom-call | tf_op jit(solution)/shard_map/slabs/pallas_call | solution.py:227
  1.3 0.0 copy-start
  1.3 0.0 copy-start.3
  1.3 0.0 copy-start.4
  1.3 18.4 %all_to_all.10.in_ref = f32[32,2,2,8,128]{4,3,2,1,0:T(8,128)S(1)} all-to-all(f32[32,2,2,8,128]{4,3,2,1,0:T(8,128)S(1)} %bitcast.8), channel_id=1, replica_groups=mesh['row'=16,'col'=32] {'col'}, dimensions={0} | all-to-all | bytes 1048576 | tf_op jit(solution)/shard_map/all_to_all | solution.py:238
  19.7 0.0 copy-done
  19.7 0.0 copy-done.3
  19.7 0.0 copy-done.4
  19.7 1.1 %transform.1 = f32[32,2,2,8,128]{4,3,2,1,0:T(8,128)S(1)} custom-call(f32[32,2,2,8,128]{4,3,2,1,0:T(8,128)S(1)} %all_to_all.10.in_ref, bf16[256,512]{1,0:T(8,128)(2,1)S(1)} %copy-done.4, bf16[256,512]{1,0:T(8,128)(2,1)S(1)} %copy-done.3, f32[2,256,256]{2,1,0:T(8,128)S(1)} %copy-done), custom_call_target="tpu_custom_call" | custom-call | tf_op jit(solution)/shard_map/transform/pallas_call | solution.py:241
  20.9 15.1 %all_to_all.11 = f32[32,2,2,8,128]{4,3,2,1,0:T(8,128)S(1)} all-to-all(f32[32,2,2,8,128]{4,3,2,1,0:T(8,128)S(1)} %transform.1), channel_id=1, replica_groups=mesh['row'=16,'col'=32] {'col'}, dimensions={0} | all-to-all | bytes 1048576 | tf_op jit(solution)/shard_map/all_to_all | solution.py:247
  35.9 0.0 copy-start.2
  36.0 3.9 %collective-permute-start = (f32[16,32,128]{2,1,0:T(8,128)S(1)}, f32[16,32,128]{2,1,0:T(8,128)S(1)}, u32[]{:S(2)}, u32[]{:S(2)}) collective-permute-start(f32[16,32,128]{2,1,0:T(8,128)S(1)} %get-tuple-element.13), channel_id=1, source_target_pairs={{0,32},{2,34},{4,36},{6,38},{8,40},{10,42},{12,44},{14,46},{16,48}... | collective-permute-start | bytes 786440 | tf_op jit(solution)/shard_map/ppermute | solution.py:217
  39.9 0.0 copy-start.6
  39.9 0.0 copy-start.5
  40.0 1.9 %collective-permute-start.1 = (f32[16,32,128]{2,1,0:T(8,128)S(1)}, f32[16,32,128]{2,1,0:T(8,128)S(1)}, u32[]{:S(2)}, u32[]{:S(2)}) collective-permute-start(f32[16,32,128]{2,1,0:T(8,128)S(1)} %get-tuple-element.16), channel_id=1, source_target_pairs={{1,33},{3,35},{5,37},{7,39},{9,41},{11,43},{13,45},{15,47},{17,49}... | collective-permute-start | bytes 786440 | tf_op jit(solution)/shard_map/ppermute | solution.py:217
  41.9 0.0 copy-done.1
  41.9 0.0 copy-done.2
  41.9 0.0 copy-done.6
  41.9 0.0 copy-done.5
  41.9 1.0 %turn.1 = (f32[32,2048]{1,0:T(8,128)S(1)}, f32[32,2048]{1,0:T(8,128)S(1)}, s32[32,128]{1,0:T(8,128)S(1)}, f32[128,128]{1,0:T(8,128)S(1)}) custom-call(s32[4,32]{1,0:T(4,128)S(1)} %bitcast.9, f32[4,32]{1,0:T(4,128)S(1)} %bitcast.10, f32[32,2048]{1,0:T(8,128)S(1)} %copy-done.1, f32[32,2048]{1,0:T(8,128)S(1)} %copy-done.2, f32[32,32,128]{2,1,0:T(8,128)S(1)} %bitcast.5), custom_call_target="tpu_custom_call" | custom-call | tf_op jit(solution)/shard_map/turn/pallas_call | solution.py:256
  42.9 1.5 %collective-permute-done.refs_3_ = f32[16,32,128]{2,1,0:T(8,128)S(1)} collective-permute-done((f32[16,32,128]{2,1,0:T(8,128)S(1)}, f32[16,32,128]{2,1,0:T(8,128)S(1)}, u32[]{:S(2)}, u32[]{:S(2)}) %collective-permute-start) | collective-permute-done | bytes 262176 | tf_op jit(solution)/shard_map/ppermute | solution.py:217
  44.4 1.0 %tilt_early.1.early_ref = f32[2,32,2048]{2,1,0:T(8,128)} custom-call(s32[32,128]{1,0:T(8,128)S(1)} %get-tuple-element.11.refs_0_, f32[128,128]{1,0:T(8,128)S(1)} %get-tuple-element.12.refs_1_, f32[32,32,128]{2,1,0:T(8,128)S(1)} %bitcast.6, f32[16,32,128]{2,1,0:T(8,128)S(1)} %collective-permute-done.refs_3_, f32[32,2048]{1,0:T(8,128)S(1)} %get-tuple-element.14.refs_4_, ...), custom_call_target="tpu_custom_call" | custom-call | tf_op jit(solution)/shard_map/tilt_early/pallas_call | solution.py:275
  45.4 4.0 %collective-permute-done.1.refs_3_ = f32[16,32,128]{2,1,0:T(8,128)S(1)} collective-permute-done((f32[16,32,128]{2,1,0:T(8,128)S(1)}, f32[16,32,128]{2,1,0:T(8,128)S(1)}, u32[]{:S(2)}, u32[]{:S(2)}) %collective-permute-start.1) | collective-permute-done | bytes 262176 | tf_op jit(solution)/shard_map/ppermute | solution.py:217
  49.4 1.0 %tilt_late.1 = f32[2,32,2048]{2,1,0:T(8,128)} custom-call(f32[2,32,2048]{2,1,0:T(8,128)} %tilt_early.1.early_ref, s32[32,128]{1,0:T(8,128)S(1)} %get-tuple-element.11.refs_0_, f32[128,128]{1,0:T(8,128)S(1)} %get-tuple-element.12.refs_1_, f32[32,32,128]{2,1,0:T(8,128)S(1)} %bitcast.7, ...), custom_call_target="tpu_custom_call", output_to_operand_aliasing={{}: (0, {})} | custom-call | tf_op jit(solution)/shard_map/tilt_late/pallas_call | solution.py:284
  (2 shorter events, 0.0 us)
Async XLA Ops:
  1.3 18.5 %copy-start = (f32[2,256,256]{2,1,0:T(8,128)S(1)}, f32[2,256,256]{2,1,0:T(8,128)}, u32[]{:S(2)}) copy-start(f32[2,256,256]{2,1,0:T(8,128)} %constant.8.clone.turn_ref) | copy-start | bytes 1572868
  1.3 18.5 %copy-start.3 = (bf16[256,512]{1,0:T(8,128)(2,1)S(1)}, bf16[256,512]{1,0:T(8,128)(2,1)}, u32[]{:S(2)}) copy-start(bf16[256,512]{1,0:T(8,128)(2,1)} %constant.7.clone.lo_ref) | copy-start | bytes 786436
  1.3 18.5 %copy-start.4 = (bf16[256,512]{1,0:T(8,128)(2,1)S(1)}, bf16[256,512]{1,0:T(8,128)(2,1)}, u32[]{:S(2)}) copy-start(bf16[256,512]{1,0:T(8,128)(2,1)} %constant.6.clone.hi_ref) | copy-start | bytes 786436
  35.9 6.0 %copy-start.1 = (f32[32,2048]{1,0:T(8,128)S(1)}, f32[32,2048]{1,0:T(8,128)}, u32[]{:S(2)}) copy-start(f32[32,2048]{1,0:T(8,128)} %jac_ref.1) | copy-start | bytes 786436
  35.9 6.0 %copy-start.2 = (f32[32,2048]{1,0:T(8,128)S(1)}, f32[32,2048]{1,0:T(8,128)}, u32[]{:S(2)}) copy-start(f32[32,2048]{1,0:T(8,128)} %phase_ref.1) | copy-start | bytes 786436
  36.0 8.4 %collective-permute-start = (f32[16,32,128]{2,1,0:T(8,128)S(1)}, f32[16,32,128]{2,1,0:T(8,128)S(1)}, u32[]{:S(2)}, u32[]{:S(2)}) collective-permute-start(f32[16,32,128]{2,1,0:T(8,128)S(1)} %get-tuple-element.13), channel_id=1, source_target_pairs={{0,32},{2,34},{4,36},{6,38},{8,40},{10,42},{12,44},{14,46},{16,48}... | collective-permute-start | bytes 786440 | tf_op jit(solution)/shard_map/ppermute | solution.py:217
  39.9 2.0 %copy-start.6 = (f32[32,4]{0,1:T(4,128)S(1)}, f32[32,4]{0,1:T(4,128)}, u32[]{:S(2)}) copy-start(f32[32,4]{0,1:T(4,128)} %param.10) | copy-start | bytes 1540
  39.9 2.0 %copy-start.5 = (s32[32,4]{0,1:T(4,128)S(1)}, s32[32,4]{0,1:T(4,128)}, u32[]{:S(2)}) copy-start(s32[32,4]{0,1:T(4,128)} %param.9) | copy-start | bytes 1540
  40.0 9.5 %collective-permute-start.1 = (f32[16,32,128]{2,1,0:T(8,128)S(1)}, f32[16,32,128]{2,1,0:T(8,128)S(1)}, u32[]{:S(2)}, u32[]{:S(2)}) collective-permute-start(f32[16,32,128]{2,1,0:T(8,128)S(1)} %get-tuple-element.16), channel_id=1, source_target_pairs={{1,33},{3,35},{5,37},{7,39},{9,41},{11,43},{13,45},{15,47},{17,49}... | collective-permute-start | bytes 786440 | tf_op jit(solution)/shard_map/ppermute | solution.py:217
